TPU v7x, 128 devices: a whole 4x4x4 slice. The times are simulated.
128 devices in a mesh: ctx: 8 (over y_lo, z), fsdp: 16 (over x, y_hi, core).
Axes of the slice: x: 4, y: 4 (y_hi: 2, y_lo: 2; y = y_hi * 2 + y_lo), z: 4, core: 2. Of those that a mesh axis runs over, the one named last changes fastest.
Arguments:
- tokens: bfloat16 [16, 2048, 1024], P('fsdp', 'ctx'), may hold values from -6 to 6
- segment_ids: int32 [16, 2048], P('fsdp', 'ctx'), may hold values from 0 to 3, never falling along the last dimension, each value on 1 to 1920 neighbouring positions
- cotangent: bfloat16 [16, 2048, 1024], P('fsdp', 'ctx'), may hold values from -6 to 6
- ln1_gain: bfloat16 [1024], P('fsdp'), may hold values from 0.099609375 to 1.8984375
- ln1_bias: bfloat16 [1024], P('fsdp'), may hold values from -3 to 3
- qkv_weight: bfloat16 [1024, 3072], P('fsdp'), may hold values from -0.1875 to 0.1875
- qkv_bias: bfloat16 [2048], P('fsdp'), may hold values from -3 to 3
- out_weight: bfloat16 [1024, 1024], P('fsdp'), may hold values from -0.5 to 0.5
- out_bias: bfloat16 [1024], P('fsdp'), may hold values from -3 to 3
- ln2_gain: bfloat16 [1024], P('fsdp'), may hold values from 0.099609375 to 1.8984375
- ln2_bias: bfloat16 [1024], P('fsdp'), may hold values from -3 to 3
- fc1_weight: bfloat16 [1024, 4096], P('fsdp'), may hold values from -0.1875 to 0.1875
- fc1_bias: bfloat16 [4096], P('fsdp'), may hold values from -3 to 3
- fc2_weight: bfloat16 [4096, 1024], P('fsdp'), may hold values from -0.125 to 0.125
- fc2_bias: bfloat16 [1024], P('fsdp'), may hold values from -3 to 3
Outputs:
- output: bfloat16 [16, 2048, 1024], P('fsdp', 'ctx')
- input_grad: float32 [16, 2048, 1024], P('fsdp', 'ctx')
- ln1_gain_grad: float32 [1024], P('fsdp')
- ln1_bias_grad: float32 [1024], P('fsdp')
- qkv_weight_grad: float32 [1024, 3072], P('fsdp')
- qkv_bias_grad: float32 [2048], P('fsdp')
- out_weight_grad: float32 [1024, 1024], P('fsdp')
- out_bias_grad: float32 [1024], P('fsdp')
- ln2_gain_grad: float32 [1024], P('fsdp')
- ln2_bias_grad: float32 [1024], P('fsdp')
- fc1_weight_grad: float32 [1024, 4096], P('fsdp')
- fc1_bias_grad: float32 [4096], P('fsdp')
- fc2_weight_grad: float32 [4096, 1024], P('fsdp')
- fc2_bias_grad: float32 [1024], P('fsdp')
- log_sum_exp: float32 [16, 16, 2048], P('fsdp', None, 'ctx')
Inputs may be any that keep to these rules, and one draw needn't show every extreme that they name: `segment_ids`: in each row the document number never falls, every document is a contiguous run of positions, and one document of each row holds exactly 1920 positions.
All inputs are finite; a program needn't handle non-finite values.
Results may differ from a plain program's by a relative error of at most 0.023.
Values may be sent and summed in bfloat16 or wider, within the bound.
A program may use at most 192 MiB of HBM per device.

v0:
```python
import jax
import jax.numpy as jnp
from jax import lax
from jax.sharding import PartitionSpec as P

D = 1024
HEADS = 16
HEAD_DIM = 64
LENGTH = 2048


def layer_norm(values, gain_vec, bias_vec):
    center = values - jnp.mean(values, axis=-1, keepdims=True)
    spread = jnp.mean(center * center, axis=-1, keepdims=True)
    return center * lax.rsqrt(spread + 1e-05) * gain_vec + bias_vec


def gelu_tanh(values):
    return jax.nn.gelu(values, approximate=True)


def matmul_tn(left, right):
    return lax.dot_general(
        left, right, (((0,), (0,)), ((), ())), preferred_element_type=jnp.float32
    )


def matmul_nt(left, right):
    return lax.dot_general(
        left, right, (((1,), (1,)), ((), ())), preferred_element_type=jnp.float32
    )


def matmul(left, right):
    return jnp.dot(left, right, preferred_element_type=jnp.float32)


def head_slopes():
    return 2.0 ** (-8.0 * jnp.arange(1, HEADS + 1, dtype=jnp.float32) / HEADS) * (4.0 / LENGTH)


def key_spans(key_count):
    width_now = 512
    return [(offset, width_now) for offset in range(0, key_count, width_now)]


def block_scores(query, query_seg, query_pos, key_rows, key_seg, first_key):
    row_count = key_rows.shape[0]
    key_count = key_rows.shape[1]
    key_part = key_rows[:, :, :D].reshape(row_count, key_count, HEADS, HEAD_DIM)
    value_part = key_rows[:, :, D:].reshape(row_count, key_count, HEADS, HEAD_DIM)
    scores = jnp.einsum(
        "rihd,rjhd->rhij", query, key_part, preferred_element_type=jnp.float32
    ) * HEAD_DIM ** (-0.5)
    key_pos = first_key + jnp.arange(key_count, dtype=jnp.int32)
    distance = query_pos[:, None] - key_pos[None, :]
    scores = scores - head_slopes()[:, None, None] * distance.astype(jnp.float32)
    allowed = (query_seg[:, :, None] == key_seg[:, None, :]) & (distance >= 0)[None]
    return (scores, allowed[:, None], key_part, value_part)


def local(
    tokens,
    segment_ids,
    cotangent,
    ln1_gain,
    ln1_bias,
    qkv_weight,
    qkv_bias,
    out_weight,
    out_bias,
    ln2_gain,
    ln2_bias,
    fc1_weight,
    fc1_bias,
    fc2_weight,
    fc2_bias,
):
    row_count, block_len, _ = tokens.shape
    flat_rows = row_count * block_len
    full_length = block_len * lax.axis_size("ctx")
    forward_full = (
        lax.all_gather(ln1_gain, "fsdp", axis=0, tiled=True),
        lax.all_gather(ln1_bias, "fsdp", axis=0, tiled=True),
        lax.all_gather(qkv_weight, "fsdp", axis=0, tiled=True),
        lax.all_gather(qkv_bias, "fsdp", axis=0, tiled=True),
        lax.all_gather(out_weight, "fsdp", axis=0, tiled=True),
        lax.all_gather(out_bias, "fsdp", axis=0, tiled=True),
        lax.all_gather(ln2_gain, "fsdp", axis=0, tiled=True),
        lax.all_gather(ln2_bias, "fsdp", axis=0, tiled=True),
        lax.all_gather(fc1_weight, "fsdp", axis=0, tiled=True),
        lax.all_gather(fc1_bias, "fsdp", axis=0, tiled=True),
        lax.all_gather(fc2_weight, "fsdp", axis=0, tiled=True),
        lax.all_gather(fc2_bias, "fsdp", axis=0, tiled=True),
    )
    (
        gain_one,
        bias_one,
        qkv_mat,
        qkv_vec,
        out_mat,
        out_vec,
        gain_two,
        bias_two,
        up_mat,
        up_vec,
        down_mat,
        down_vec,
    ) = forward_full
    gain_one_f = gain_one.astype(jnp.float32)
    bias_one_f = bias_one.astype(jnp.float32)
    gain_two_f = gain_two.astype(jnp.float32)
    bias_two_f = bias_two.astype(jnp.float32)
    inputs = tokens.astype(jnp.float32).reshape(flat_rows, D)
    normed = layer_norm(inputs, gain_one_f, bias_one_f).astype(jnp.bfloat16)
    qkv_float = qkv_vec.astype(jnp.float32)
    merged_bias = jnp.concatenate([qkv_float[:D], jnp.zeros((D,), jnp.float32), qkv_float[D:]])
    merged = (matmul(normed, qkv_mat) + merged_bias).astype(jnp.bfloat16)
    query = merged[:, :D].reshape(row_count, block_len, HEADS, HEAD_DIM)
    key_values = merged[:, D:].reshape(row_count, block_len, 2 * D)
    query_pos = lax.axis_index("ctx") * block_len + jnp.arange(block_len, dtype=jnp.int32)
    first_row = jnp.int32(0)
    running_top = jnp.full((row_count, HEADS, block_len), -1e30, jnp.float32)
    running_sum = jnp.zeros((row_count, HEADS, block_len), jnp.float32)
    weighted = jnp.zeros((row_count, block_len, HEADS, HEAD_DIM), jnp.float32)
    key_rows = lax.all_gather(key_values, "ctx", axis=1, tiled=True)
    key_seg = lax.all_gather(segment_ids, "ctx", axis=1, tiled=True)
    for offset, width_now in key_spans(key_rows.shape[1]):
        scores, allowed, key_part, value_part = block_scores(
            query,
            segment_ids,
            query_pos,
            key_rows[:, offset : offset + width_now],
            key_seg[:, offset : offset + width_now],
            first_row + offset,
        )
        masked = jnp.where(allowed, scores, -1e30)
        new_top = jnp.maximum(running_top, jnp.max(masked, axis=-1))
        fade_out = jnp.exp(running_top - new_top)
        expo = jnp.where(allowed, jnp.exp(scores - new_top[..., None]), 0.0)
        running_sum = running_sum * fade_out + jnp.sum(expo, axis=-1)
        weighted = weighted * jnp.swapaxes(fade_out, 1, 2)[..., None] + jnp.einsum(
            "rhij,rjhd->rihd",
            expo.astype(jnp.bfloat16),
            value_part,
            preferred_element_type=jnp.float32,
        )
        running_top = new_top
    final_top, final_sum, weighted = (running_top, running_sum, weighted)
    log_sums = final_top + jnp.log(final_sum)
    mixed_exact = weighted / jnp.swapaxes(final_sum, 1, 2)[..., None]
    mixed = mixed_exact.astype(jnp.bfloat16).reshape(flat_rows, D)
    middle = inputs + matmul(mixed, out_mat) + out_vec.astype(jnp.float32)
    normed_two = layer_norm(middle, gain_two_f, bias_two_f).astype(jnp.bfloat16)
    hidden = matmul(normed_two, up_mat) + up_vec.astype(jnp.float32)
    active = gelu_tanh(hidden).astype(jnp.bfloat16)
    output = middle + matmul(active, down_mat) + down_vec.astype(jnp.float32)
    back_full = (
        lax.all_gather(ln1_gain, "fsdp", axis=0, tiled=True),
        lax.all_gather(ln1_bias, "fsdp", axis=0, tiled=True),
        lax.all_gather(qkv_weight, "fsdp", axis=0, tiled=True),
        lax.all_gather(qkv_bias, "fsdp", axis=0, tiled=True),
        lax.all_gather(out_weight, "fsdp", axis=0, tiled=True),
        lax.all_gather(out_bias, "fsdp", axis=0, tiled=True),
        lax.all_gather(ln2_gain, "fsdp", axis=0, tiled=True),
        lax.all_gather(ln2_bias, "fsdp", axis=0, tiled=True),
        lax.all_gather(fc1_weight, "fsdp", axis=0, tiled=True),
        lax.all_gather(fc1_bias, "fsdp", axis=0, tiled=True),
        lax.all_gather(fc2_weight, "fsdp", axis=0, tiled=True),
        lax.all_gather(fc2_bias, "fsdp", axis=0, tiled=True),
    )
    _, _, qkv_back, _, out_back, _, _, _, up_back, _, down_back, _ = back_full
    grad_down = cotangent.reshape(flat_rows, D)
    grad_output = grad_down.astype(jnp.float32)
    fc2_weight_grad = matmul_tn(active, grad_down)
    fc2_bias_grad = jnp.sum(grad_output, axis=0)
    grad_active = matmul_nt(grad_down, down_back)
    _, gelu_pull = jax.vjp(gelu_tanh, hidden)
    grad_hidden = gelu_pull(grad_active)[0].astype(jnp.bfloat16)
    fc1_weight_grad = matmul_tn(normed_two, grad_hidden)
    fc1_bias_grad = jnp.sum(grad_hidden.astype(jnp.float32), axis=0)
    grad_normed_two = matmul_nt(grad_hidden, up_back)
    _, norm_pull_two = jax.vjp(layer_norm, middle, gain_two_f, bias_two_f)
    grad_middle_part, ln2_gain_grad, ln2_bias_grad = norm_pull_two(grad_normed_two)
    grad_middle = grad_output + grad_middle_part
    grad_branch = grad_middle.astype(jnp.bfloat16)
    out_weight_grad = matmul_tn(mixed, grad_branch)
    out_bias_grad = jnp.sum(grad_branch.astype(jnp.float32), axis=0)
    grad_mixed = (
        matmul_nt(grad_branch, out_back)
        .astype(jnp.bfloat16)
        .reshape(row_count, block_len, HEADS, HEAD_DIM)
    )
    delta = jnp.swapaxes(jnp.sum(grad_mixed.astype(jnp.float32) * mixed_exact, axis=-1), 1, 2)
    first_row = jnp.int32(0)
    grad_query = jnp.zeros((row_count, block_len, HEADS, HEAD_DIM), jnp.float32)
    grad_keys = jnp.zeros((row_count, full_length, 2 * D), jnp.float32)
    key_rows = lax.all_gather(key_values, "ctx", axis=1, tiled=True)
    key_seg = lax.all_gather(segment_ids, "ctx", axis=1, tiled=True)
    for offset, width_now in key_spans(key_rows.shape[1]):
        scores, allowed, key_part, value_part = block_scores(
            query,
            segment_ids,
            query_pos,
            key_rows[:, offset : offset + width_now],
            key_seg[:, offset : offset + width_now],
            first_row + offset,
        )
        probs = jnp.where(allowed, jnp.exp(scores - log_sums[..., None]), 0.0)
        grad_probs = jnp.einsum(
            "rihd,rjhd->rhij", grad_mixed, value_part, preferred_element_type=jnp.float32
        )
        grad_scores = (probs * (grad_probs - delta[..., None])).astype(jnp.bfloat16)
        grad_query = grad_query + jnp.einsum(
            "rhij,rjhd->rihd", grad_scores, key_part, preferred_element_type=jnp.float32
        ) * HEAD_DIM ** (-0.5)
        grad_key = jnp.einsum(
            "rhij,rihd->rjhd", grad_scores, query, preferred_element_type=jnp.float32
        ) * HEAD_DIM ** (-0.5)
        grad_value = jnp.einsum(
            "rhij,rihd->rjhd",
            probs.astype(jnp.bfloat16),
            grad_mixed,
            preferred_element_type=jnp.float32,
        )
        key_term = jnp.concatenate(
            [
                grad_key.reshape(row_count, width_now, D),
                grad_value.reshape(row_count, width_now, D),
            ],
            axis=-1,
        )
        place_at = first_row + offset
        previous = lax.dynamic_slice_in_dim(grad_keys, place_at, width_now, 1)
        grad_keys = lax.dynamic_update_slice_in_dim(grad_keys, previous + key_term, place_at, 1)
    grad_query, grad_keys = (grad_query, grad_keys)
    own_key_grads = lax.psum_scatter(
        grad_keys.astype(jnp.bfloat16), "ctx", scatter_dimension=1, tiled=True
    ).astype(jnp.float32)
    grad_merged = jnp.concatenate(
        [grad_query.reshape(flat_rows, D), own_key_grads.reshape(flat_rows, 2 * D)], axis=-1
    ).astype(jnp.bfloat16)
    qkv_weight_grad = matmul_tn(normed, grad_merged)
    merged_sums = jnp.sum(grad_merged.astype(jnp.float32), axis=0)
    qkv_bias_grad = jnp.concatenate([merged_sums[:D], merged_sums[2 * D :]])
    grad_normed = matmul_nt(grad_merged, qkv_back)
    _, norm_pull_one = jax.vjp(layer_norm, inputs, gain_one_f, bias_one_f)
    grad_input_part, ln1_gain_grad, ln1_bias_grad = norm_pull_one(grad_normed)
    input_grad = (grad_middle + grad_input_part).reshape(row_count, block_len, D)
    shard_grads = (
        lax.psum_scatter(
            ln1_gain_grad.astype(jnp.bfloat16), "fsdp", scatter_dimension=0, tiled=True
        ).astype(jnp.float32),
        lax.psum_scatter(
            ln1_bias_grad.astype(jnp.bfloat16), "fsdp", scatter_dimension=0, tiled=True
        ).astype(jnp.float32),
        lax.psum_scatter(
            qkv_weight_grad.astype(jnp.bfloat16), "fsdp", scatter_dimension=0, tiled=True
        ).astype(jnp.float32),
        lax.psum_scatter(
            qkv_bias_grad.astype(jnp.bfloat16), "fsdp", scatter_dimension=0, tiled=True
        ).astype(jnp.float32),
        lax.psum_scatter(
            out_weight_grad.astype(jnp.bfloat16), "fsdp", scatter_dimension=0, tiled=True
        ).astype(jnp.float32),
        lax.psum_scatter(
            out_bias_grad.astype(jnp.bfloat16), "fsdp", scatter_dimension=0, tiled=True
        ).astype(jnp.float32),
        lax.psum_scatter(
            ln2_gain_grad.astype(jnp.bfloat16), "fsdp", scatter_dimension=0, tiled=True
        ).astype(jnp.float32),
        lax.psum_scatter(
            ln2_bias_grad.astype(jnp.bfloat16), "fsdp", scatter_dimension=0, tiled=True
        ).astype(jnp.float32),
        lax.psum_scatter(
            fc1_weight_grad.astype(jnp.bfloat16), "fsdp", scatter_dimension=0, tiled=True
        ).astype(jnp.float32),
        lax.psum_scatter(
            fc1_bias_grad.astype(jnp.bfloat16), "fsdp", scatter_dimension=0, tiled=True
        ).astype(jnp.float32),
        lax.psum_scatter(
            fc2_weight_grad.astype(jnp.bfloat16), "fsdp", scatter_dimension=0, tiled=True
        ).astype(jnp.float32),
        lax.psum_scatter(
            fc2_bias_grad.astype(jnp.bfloat16), "fsdp", scatter_dimension=0, tiled=True
        ).astype(jnp.float32),
    )
    g_one, b_one, g_qkv, g_qkvb, g_out, g_outb, g_two, b_two, g_up, g_upb, g_down, g_downb = (
        lax.psum(shard_grads[0].astype(jnp.bfloat16), "ctx").astype(jnp.float32),
        lax.psum(shard_grads[1].astype(jnp.bfloat16), "ctx").astype(jnp.float32),
        lax.psum(shard_grads[2].astype(jnp.bfloat16), "ctx").astype(jnp.float32),
        lax.psum(shard_grads[3].astype(jnp.bfloat16), "ctx").astype(jnp.float32),
        lax.psum(shard_grads[4].astype(jnp.bfloat16), "ctx").astype(jnp.float32),
        lax.psum(shard_grads[5].astype(jnp.bfloat16), "ctx").astype(jnp.float32),
        lax.psum(shard_grads[6].astype(jnp.bfloat16), "ctx").astype(jnp.float32),
        lax.psum(shard_grads[7].astype(jnp.bfloat16), "ctx").astype(jnp.float32),
        lax.psum(shard_grads[8].astype(jnp.bfloat16), "ctx").astype(jnp.float32),
        lax.psum(shard_grads[9].astype(jnp.bfloat16), "ctx").astype(jnp.float32),
        lax.psum(shard_grads[10].astype(jnp.bfloat16), "ctx").astype(jnp.float32),
        lax.psum(shard_grads[11].astype(jnp.bfloat16), "ctx").astype(jnp.float32),
    )
    return (
        output.astype(jnp.bfloat16).reshape(row_count, block_len, D),
        input_grad,
        g_one,
        b_one,
        g_qkv,
        g_qkvb,
        g_out,
        g_outb,
        g_two,
        b_two,
        g_up,
        g_upb,
        g_down,
        g_downb,
        log_sums,
    )


def solution(mesh):
    placed = (
        P("fsdp", "ctx", None),
        P("fsdp", "ctx"),
        P("fsdp", "ctx", None),
        P("fsdp"),
        P("fsdp"),
        P("fsdp", None),
        P("fsdp"),
        P("fsdp", None),
        P("fsdp"),
        P("fsdp"),
        P("fsdp"),
        P("fsdp", None),
        P("fsdp"),
        P("fsdp", None),
        P("fsdp"),
    )
    return jax.shard_map(
        local,
        mesh=mesh,
        in_specs=placed,
        out_specs=(
            P("fsdp", "ctx", None),
            P("fsdp", "ctx", None),
            P("fsdp"),
            P("fsdp"),
            P("fsdp", None),
            P("fsdp"),
            P("fsdp", None),
            P("fsdp"),
            P("fsdp"),
            P("fsdp"),
            P("fsdp", None),
            P("fsdp"),
            P("fsdp", None),
            P("fsdp"),
            P("fsdp", None, "ctx"),
        ),
        check_vma=False,
    )
```

profile of v0, /device:TPU:0, one launch (start us, length us, event | category | flops | bytes accessed | tf_op | source)
XLA Modules:
  0.0 1079.2 jit_solution(6444163785159172007)
XLA Ops:
  14.1 70.2 %all-reduce.16 = (bf16[1024]{0:T(1024)(128)(2,1)S(1)}, bf16[1024]{0:T(1024)(128)(2,1)S(1)}, bf16[1024]{0:T(1024)(128)(2,1)S(1)}, bf16[1024]{0:T(1024)(128)(2,1)S(1)}, bf16[1024]{0:T(1024)(128)(2,1)S(1)}) all-reduce(bf16[1024]{0:T(1024)(128)(2,1)S(1)} %dynamic-update-slice.1, ...), channel_id=1, replica_groups=mesh['ctx'=8,'fsdp'=16] {'fsdp'}, use_global_device_ids=true, to_apply=%add.2 | all-reduce | flops 5120 | bytes 20480
  84.4 19.1 %all-gather.1 = bf16[16,1,128]{2,1,0:T(2,128)(2,1)S(1)} all-gather(bf16[1,1,128]{2,1,0:T(2,128)(2,1)} %bitcast.393), channel_id=1, replica_groups=mesh['ctx'=8,'fsdp'=16] {'fsdp'}, dimensions={0}, use_global_device_ids=true | all-gather | bytes 4352 | tf_op jit(solution)/shard_map/all_gather | solution.py:86
  115.8 22.3 %all-gather.2 = bf16[16,1,256]{2,1,0:T(2,128)(2,1)S(1)} all-gather(bf16[1,1,256]{2,1,0:T(2,128)(2,1)S(1)} %reshape.1157), channel_id=1, replica_groups=mesh['ctx'=8,'fsdp'=16] {'fsdp'}, dimensions={0}, use_global_device_ids=true | all-gather | bytes 8704 | tf_op jit(solution)/shard_map/all_gather | solution.py:92
  138.7 19.3 %all_gather.48 = s32[1,2048]{1,0:T(1,128)S(1)} all-gather(s32[1,256]{1,0:T(1,128)S(1)} %copy-done.72), channel_id=1, replica_groups=mesh['ctx'=8,'fsdp'=16] {'ctx'}, dimensions={1}, use_global_device_ids=true | all-gather | bytes 9216 | tf_op jit(solution)/shard_map/all_gather | solution.py:127
  160.5 45.0 %all-gather.17.cloned.1.call-done = bf16[2048,2048]{1,0:T(8,128)(2,1)} async-done(((bf16[256,2048]{1,0:T(8,128)(2,1)}), bf16[2048,2048]{1,0:T(8,128)(2,1)}) %all-gather.17.cloned.1.call-update) | async-done | bytes 8388624 | tf_op jit(solution)/shard_map/all_gather | solution.py:126
  205.4 6.2 fusion.162
  233.4 5.9 select_reduce_fusion
  242.1 5.6 fusion
  247.7 6.8 fusion.4
  270.1 58.4 %all-gather.13.cloned.1.call-done = bf16[1024,4096]{1,0:T(8,128)(2,1)} async-done(((bf16[64,4096]{1,0:T(8,128)(2,1)}), bf16[1024,4096]{1,0:T(8,128)(2,1)}) %all-gather.13.cloned.1.call-update) | async-done | bytes 8388624 | tf_op jit(solution)/shard_map/all_gather | solution.py:91
  328.5 7.9 convolution_add_fusion
  336.4 64.9 %all-gather.15.cloned.1.call-done = bf16[4096,1024]{1,0:T(8,128)(2,1)} async-done(((bf16[256,1024]{1,0:T(8,128)(2,1)}), bf16[4096,1024]{1,0:T(8,128)(2,1)}) %all-gather.15.cloned.1.call-update) | async-done | bytes 8388624 | tf_op jit(solution)/shard_map/all_gather | solution.py:93
  401.3 12.3 %fusion.169 = (bf16[4096]{0:T(1024)(128)(2,1)}, bf16[256,4096]{1,0:T(8,128)(2,1)S(1)}) fusion(f32[256,4096]{1,0:T(8,128)} %convolution_add_fusion, bf16[4096,1024]{1,0:T(8,128)(2,1)} %all-gather.15.cloned.1.call-done, bf16[1,256,1024]{2,1,0:T(8,128)(2,1)S(1)} %copy-done.21), kind=kOutput, calls=%fused_computation.223 | convolution fusion | flops 2169499648 | bytes 15212544 | tf_op jit(solution)/shard_map/dot_general | solution.py:29
  424.9 5.9 fusion.19
  430.9 5.9 fusion.21
  464.3 7.4 select_maximum_fusion
  471.7 4.9 maximum_dynamic-update-slice_fusion
  476.6 5.4 fusion.36
  482.0 5.2 fusion.35
  487.2 9.0 convert_element_type.286
  500.0 7.4 convolution_convert_fusion.1
  507.4 8.5 convolution_convert_fusion
  526.5 60.6 %reduce-scatter.6.cloned.1.call-done = bf16[1,256,2048]{1,2,0:T(8,128)(2,1)} async-done(((bf16[1,2048,2048]{1,2,0:T(8,128)(2,1)}), bf16[1,256,2048]{1,2,0:T(8,128)(2,1)}) %reduce-scatter.6.cloned.1.call-update) | async-done | bytes 1048592 | tf_op jit(solution)/shard_map/reduce_scatter | solution.py:237
  587.2 6.0 convolution_convert_fusion.2
  597.5 5.5 fusion.156
  604.6 56.0 %reduce-scatter.10.cloned.1.call-done = bf16[64,1024]{1,0:T(8,128)(2,1)} async-done(((bf16[1024,1024]{1,0:T(8,128)(2,1)}), bf16[64,1024]{1,0:T(8,128)(2,1)}) %reduce-scatter.10.cloned.1.call-update) | async-done | bytes 131088 | tf_op jit(solution)/shard_map/reduce_scatter | solution.py:263
  660.6 106.0 %reduce-scatter.12.cloned.1.call-done = bf16[64,4096]{1,0:T(8,128)(2,1)} async-done(((bf16[1024,4096]{1,0:T(8,128)(2,1)}), bf16[64,4096]{1,0:T(8,128)(2,1)}) %reduce-scatter.12.cloned.1.call-update) | async-done | bytes 524304 | tf_op jit(solution)/shard_map/reduce_scatter | solution.py:275
  766.6 105.7 %reduce-scatter.14.cloned.1.call-done = bf16[256,1024]{1,0:T(8,128)(2,1)} async-done(((bf16[4096,1024]{1,0:T(8,128)(2,1)}), bf16[256,1024]{1,0:T(8,128)(2,1)}) %reduce-scatter.14.cloned.1.call-update) | async-done | bytes 524304 | tf_op jit(solution)/shard_map/reduce_scatter | solution.py:281
  872.3 92.4 %reduce-scatter.8.cloned.1.call-done = bf16[64,3072]{1,0:T(8,128)(2,1)} async-done(((bf16[1024,3072]{1,0:T(8,128)(2,1)}), bf16[64,3072]{1,0:T(8,128)(2,1)}) %reduce-scatter.8.cloned.1.call-update) | async-done | bytes 393232 | tf_op jit(solution)/shard_map/reduce_scatter | solution.py:257
  964.8 65.8 %all-reduce.15 = (bf16[1024]{0:T(1024)(128)(2,1)S(1)}, bf16[1024]{0:T(1024)(128)(2,1)S(1)}, bf16[1024]{0:T(1024)(128)(2,1)S(1)}, bf16[2048]{0:T(1024)(128)(2,1)S...) all-reduce(bf16[1024]{0:T(1024)(128)(2,1)S(1)} %dynamic-update-slic, ...), channel_id=1, replica_groups=mesh['ctx'=8,'fsdp'=16] {'fsdp'}, use_global_device_ids=true, to_apply=%add.6 | all-reduce | flops 13312 | bytes 53248
  1031.2 19.7 %all-reduce.17 = (bf16[64]{0:T(256)(128)(2,1)S(1)}, bf16[64]{0:T(256)(128)(2,1)S(1)}, bf16[128]{0:T(256)(128)(2,1)S(1)}, bf16[64]{0:T(256)(128)(2,1)S(1)}, bf16[...) all-reduce(bf16[64]{0:T(256)(128)(2,1)S(1)} %dynamic-slice.7, ...), channel_id=1, replica_groups=mesh['ctx'=8,'fsdp'=16] {'ctx'}, use_global_device_ids=true, to_apply=%region_20.21 | all-reduce | flops 768 | bytes 3072 | tf_op jit(solution)/shard_map/psum | solution.py:289
  1057.8 7.0 fusion.105
  (322 shorter events, 133.0 us)
Async XLA Ops:
  7.2 99.4 %all-gather.9.cloned.1.call-start = ((), (), s32[]{:S(2)}) async-start(), calls=%async_computation.5 | async-start | bytes 6684672 | tf_op jit(solution)/shard_map/all_gather | solution.py:85
  7.9 197.5 %all-gather.17.cloned.1.call-start = ((), (), s32[]{:S(2)}) async-start(), calls=%async_computation.14 | async-start | bytes 9437184 | tf_op jit(solution)/shard_map/all_gather | solution.py:126
  111.5 27.2 %copy-start.72 = (s32[1,256]{1,0:T(1,128)S(1)}, s32[1,256]{1,0:T(1,128)}, u32[]{:S(2)}) copy-start(s32[1,256]{1,0:T(1,128)} %param.16) | copy-start | bytes 3076
  112.6 154.0 %all-gather.11.cloned.1.call-start = ((), (), s32[]{:S(2)}) async-start(), calls=%async_computation.6 | async-start | bytes 2228224 | tf_op jit(solution)/shard_map/all_gather | solution.py:87
  113.4 215.1 %all-gather.13.cloned.1.call-start = ((), (), s32[]{:S(2)}) async-start(), calls=%async_computation.7 | async-start | bytes 8912896 | tf_op jit(solution)/shard_map/all_gather | solution.py:91
  113.9 287.4 %all-gather.15.cloned.1.call-start = ((), (), s32[]{:S(2)}) async-start(), calls=%async_computation.8 | async-start | bytes 8912896 | tf_op jit(solution)/shard_map/all_gather | solution.py:93
  114.5 472.6 %reduce-scatter.6.cloned.1.call-start = ((), (), s32[]{:S(2)}) async-start(), calls=%async_computation.9 | async-start | bytes 9437184 | tf_op jit(solution)/shard_map/reduce_scatter | solution.py:237
  158.7 104.4 %copy-start.36 = (pred[256,512]{1,0:T(8,128)(4,1)}, pred[256,512]{1,0:T(8,128)(4,1)S(1)}, u32[]{:S(2)}) copy-start(pred[256,512]{1,0:T(8,128)(4,1)S(1)} %get-tuple-element.80) | copy-start | bytes 393220
  216.8 44.4 %copy-start.15 = (bf16[1,512,1024]{1,2,0:T(8,128)(2,1)}, bf16[1,512,1024]{1,2,0:T(8,128)(2,1)S(1)}, u32[]{:S(2)}) copy-start(bf16[1,512,1024]{1,2,0:T(8,128)(2,1)S(1)} %copy.80) | copy-start | bytes 3145732
  219.6 38.3 %copy-start.13 = (bf16[1,512,1024]{1,2,0:T(8,128)(2,1)}, bf16[1,512,1024]{1,2,0:T(8,128)(2,1)S(1)}, u32[]{:S(2)}) copy-start(bf16[1,512,1024]{1,2,0:T(8,128)(2,1)S(1)} %copy.78) | copy-start | bytes 3145732
  230.7 30.5 %copy-start.1 = (f32[16,256,512]{2,1,0:T(8,128)}, f32[16,256,512]{2,1,0:T(8,128)S(1)}, u32[]{:S(2)}) copy-start(f32[16,256,512]{2,1,0:T(8,128)S(1)} %get-tuple-element.91) | copy-start | bytes 25165828
  266.6 69.8 %copy-start.40 = (bf16[1,256,16,64]{1,3,2,0:T(8,128)(2,1)}, bf16[1,256,16,64]{1,3,2,0:T(8,128)(2,1)S(1)}, u32[]{:S(2)}) copy-start(bf16[1,256,16,64]{1,3,2,0:T(8,128)(2,1)S(1)} %get-tuple-element.96) | copy-start | bytes 1572868
  269.2 59.3 %copy-start.59 = (f32[256]{0:T(256)}, f32[256]{0:T(256)S(1)}, u32[]{:S(2)}) copy-start(f32[256]{0:T(256)S(1)} %broadcast_multiply_fusion) | copy-start | bytes 3076
  269.5 59.0 %copy-start.68 = (f32[256]{0:T(256)}, f32[256]{0:T(256)S(1)}, u32[]{:S(2)}) copy-start(f32[256]{0:T(256)S(1)} %multiply_reduce_fusion.3) | copy-start | bytes 3076
  328.5 72.8 %copy-start.21 = (bf16[1,256,1024]{2,1,0:T(8,128)(2,1)S(1)}, bf16[1,256,1024]{2,1,0:T(8,128)(2,1)}, u32[]{:S(2)}) copy-start(bf16[1,256,1024]{2,1,0:T(8,128)(2,1)} %param.17) | copy-start | bytes 1572868
  496.3 164.3 %reduce-scatter.10.cloned.1.call-start = ((), (), s32[]{:S(2)}) async-start(), calls=%async_computation.11 | async-start | bytes 2228224 | tf_op jit(solution)/shard_map/reduce_scatter | solution.py:263
  499.5 267.1 %reduce-scatter.12.cloned.1.call-start = ((), (), s32[]{:S(2)}) async-start(), calls=%async_computation.12 | async-start | bytes 8912896 | tf_op jit(solution)/shard_map/reduce_scatter | solution.py:275
  507.4 364.9 %reduce-scatter.14.cloned.1.call-start = ((), (), s32[]{:S(2)}) async-start(), calls=%async_computation.13 | async-start | bytes 8912896 | tf_op jit(solution)/shard_map/reduce_scatter | solution.py:281
  515.9 448.8 %reduce-scatter.8.cloned.1.call-start = ((), (), s32[]{:S(2)}) async-start(), calls=%async_computation.10 | async-start | bytes 6684672 | tf_op jit(solution)/shard_map/reduce_scatter | solution.py:257
  525.1 62.0 %copy-start.49 = (f32[1024]{0:T(1024)S(1)}, f32[1024]{0:T(1024)}, u32[]{:S(2)}) copy-start(f32[1024]{0:T(1024)} %copy-done.48) | copy-start | bytes 12292
  525.1 62.0 %copy-start.53 = (f32[1024]{0:T(1024)S(1)}, f32[1024]{0:T(1024)}, u32[]{:S(2)}) copy-start(f32[1024]{0:T(1024)} %copy-done.52) | copy-start | bytes 12292
  525.1 62.0 %copy-start.56 = (f32[256]{0:T(256)S(1)}, f32[256]{0:T(256)}, u32[]{:S(2)}) copy-start(f32[256]{0:T(256)} %copy-done.55) | copy-start | bytes 3076
  525.1 62.0 %copy-start.58 = (f32[256]{0:T(256)S(1)}, f32[256]{0:T(256)}, u32[]{:S(2)}) copy-start(f32[256]{0:T(256)} %copy-done.57) | copy-start | bytes 3076
  526.5 69.2 %copy-start.23 = (bf16[16,64,256]{2,1,0:T(8,128)(2,1)}, bf16[16,64,256]{2,1,0:T(8,128)(2,1)S(1)}, u32[]{:S(2)}) copy-start(bf16[16,64,256]{2,1,0:T(8,128)(2,1)S(1)} %fusion.104) | copy-start | bytes 1572868
  593.2 471.5 %all-reduce.21.cloned.1.call-start = ((), (), s32[]{:S(2)}) async-start(), calls=%async_computation.15 | async-start | bytes 3145728 | tf_op jit(solution)/shard_map/psum | solution.py:291
  597.4 367.4 %copy-start.70 = (bf16[1024]{0:T(1024)(128)(2,1)S(1)}, bf16[1024]{0:T(1024)(128)(2,1)}, u32[]{:S(2)}) copy-start(bf16[1024]{0:T(1024)(128)(2,1)} %get-tuple-element.50) | copy-start | bytes 6148
  597.4 367.4 %copy-start.71 = (bf16[4096]{0:T(1024)(128)(2,1)S(1)}, bf16[4096]{0:T(1024)(128)(2,1)}, u32[]{:S(2)}) copy-start(bf16[4096]{0:T(1024)(128)(2,1)} %get-tuple-element.102) | copy-start | bytes 24580
  597.5 367.4 %copy-start.73 = (bf16[1024]{0:T(1024)(128)(2,1)S(1)}, bf16[1024]{0:T(1024)(128)(2,1)}, u32[]{:S(2)}) copy-start(bf16[1024]{0:T(1024)(128)(2,1)} %get-tuple-element.15) | copy-start | bytes 6148
  597.5 367.4 %copy-start.74 = (bf16[1024]{0:T(1024)(128)(2,1)S(1)}, bf16[1024]{0:T(1024)(128)(2,1)}, u32[]{:S(2)}) copy-start(bf16[1024]{0:T(1024)(128)(2,1)} %get-tuple-element.19) | copy-start | bytes 6148
  597.5 457.6 %copy-start.12 = (f32[256,1024]{1,0:T(8,128)S(1)}, f32[256,1024]{1,0:T(8,128)}, u32[]{:S(2)}) copy-start(f32[256,1024]{1,0:T(8,128)} %copy-done.11) | copy-start | bytes 3145732
  597.5 457.6 %copy-start.22 = (bf16[1,256,1024]{2,1,0:T(8,128)(2,1)S(1)}, bf16[1,256,1024]{2,1,0:T(8,128)(2,1)}, u32[]{:S(2)}) copy-start(bf16[1,256,1024]{2,1,0:T(8,128)(2,1)} %param.17) | copy-start | bytes 1572868
  597.5 457.6 %copy-start.65 = (f32[256]{0:T(256)S(1)}, f32[256]{0:T(256)}, u32[]{:S(2)}) copy-start(f32[256]{0:T(256)} %copy-done.64) | copy-start | bytes 3076
  (68 other events, 413.8 us)
Sparse Core Ops, SparseCore 0:
  10.4 66.9 all-gather.8
  112.7 92.6 all-gather.16
  207.8 46.7 all-gather.10
  256.9 71.5 all-gather.12
  330.7 70.5 all-gather.14
  496.4 90.7 reduce-scatter.5
  591.1 69.4 reduce-scatter.9
  664.9 101.6 reduce-scatter.11
  770.9 101.3 reduce-scatter.13
  876.3 88.4 reduce-scatter.7
  967.5 79.3 all-reduce.20
where the time goes:
time: 1080 us
  waiting for transfers between devices  592 us (55%)
  blocking collectives  216 us (20%)
  matrix products  141 us (13%)
  other arithmetic  70.7 us (7%)
  local copies, waits for them, and re-layouts  40.5 us (4%)
  between operations  17.8 us (2%)
    unnamed x2, blocking collectives  136 us
    reduce_scatter x1, waiting for transfers between devices, local(): lax.psum_scatter(fc1_weight_grad.astype(jnp.bfloat16), 'fsdp', scatter_di...  106 us
    reduce_scatter x1, waiting for transfers between devices, local(): lax.psum_scatter(fc2_weight_grad.astype(jnp.bfloat16), 'fsdp', scatter_di...  106 us
    reduce_scatter x1, waiting for transfers between devices, local(): lax.psum_scatter(qkv_weight_grad.astype(jnp.bfloat16), 'fsdp', scatter_di...  92.4 us
    all_gather x1, waiting for transfers between devices, local(): lax.all_gather(fc2_weight, 'fsdp', axis=0, tiled=True)  64.9 us
    reduce_scatter x1, waiting for transfers between devices, local(): lax.psum_scatter(grad_keys.astype(jnp.bfloat16), 'ctx', scatter_dimension...  60.6 us
    all_gather x1, waiting for transfers between devices, local(): lax.all_gather(fc1_weight, 'fsdp', axis=0, tiled=True)  58.4 us
    reduce_scatter x1, waiting for transfers between devices, local(): lax.psum_scatter(out_weight_grad.astype(jnp.bfloat16), 'fsdp', scatter_di...  56 us
  transfers between devices with their start and end apart: 11, of which 8 were waited for; matrix products, arithmetic and copies ran while one was open for 13% of the time, Pallas kernels for 0%

commit v1 on v0

--- a/solution.py
+++ b/solution.py
@@ -1,12 +1,465 @@
+import functools
+
 import jax
 import jax.numpy as jnp
 from jax import lax
+from jax.experimental import pallas as pl
+from jax.experimental.pallas import tpu as pltpu
 from jax.sharding import PartitionSpec as P
 
 D = 1024
 HEADS = 16
 HEAD_DIM = 64
 LENGTH = 2048
+BLK = 256
+BF = jnp.bfloat16
+F32 = jnp.float32
+BIG = 2.0**100
+MIB = 2**20
+NONE = slice(None)
+
+QKV_SEGS = ((0, 0, 0, 1), (0, 1, 1, 1), (0, 2, 2, 1))
+REST_SEGS = (
+    (1, 0, 0, 1),
+    (2, 0, 0, 2),
+    (2, 1, 2, 1),
+    (2, 2, 3, 1),
+    (3, 0, 0, 1),
+    (3, 1, 1, 1),
+    (3, 2, 2, 2),
+)
+
+
+def place():
+    c = lax.axis_index("ctx")
+    f = lax.axis_index("fsdp")
+    return f // 4, ((f // 2) % 2) * 2 + c // 4, c % 4, f % 2
+
+
+def device(x, y, z, core):
+    return {"ctx": (y % 2) * 4 + z, "fsdp": x * 4 + (y // 2) * 2 + core}
+
+
+class Links:
+    def __init__(self, send, recv):
+        self.send, self.recv, self.used = send, recv, 0
+        self.x, self.y, self.z, self.core = place()
+        self.yh, self.yl = self.y // 2, self.y % 2
+        self.me = self.yl * 4 + self.z
+
+    def peers(self, axis):
+        x, y, z, c = self.x, self.y, self.z, self.core
+        if axis == "x":
+            return [device((x + j) % 4, y, z, c) for j in (1, 2, 3)]
+        if axis == "y":
+            return [device(x, (y + j) % 4, z, c) for j in (1, 2, 3)]
+        if axis == "z":
+            return [device(x, y, (z + j) % 4, c) for j in (1, 2, 3)]
+        return [device(x, y, z, 1 - c)]
+
+    def rows_peers(self):
+        out = []
+        for j in range(1, 8):
+            t = (self.me + j) % 8
+            out.append((t, device(self.x, self.yh * 2 + t // 4, t % 4, self.core)))
+        return out
+
+    def barrier(self):
+        everyone = self.peers("x") + self.peers("y") + self.peers("z") + self.peers("core")
+        for j in (1, 2, 3):
+            everyone.append(device(self.x, self.yh * 2 + 1 - self.yl, (self.z + j) % 4, self.core))
+        sem = pltpu.get_barrier_semaphore()
+        for who in everyone:
+            pl.semaphore_signal(sem, inc=1, device_id=who)
+        pl.semaphore_wait(sem, len(everyone))
+
+    def to(self, src, dst, who):
+        i = self.used
+        self.used += 1
+        copy = pltpu.make_async_remote_copy(
+            src_ref=src,
+            dst_ref=dst,
+            send_sem=self.send.at[i],
+            recv_sem=self.recv.at[i],
+            device_id=who,
+        )
+        copy.start()
+        return copy
+
+    def local(self, src, dst):
+        i = self.used
+        self.used += 1
+        copy = pltpu.make_async_copy(src, dst, self.send.at[i])
+        copy.start()
+        return copy
+
+
+def wait_recv(copies):
+    for copy in copies:
+        copy.wait_recv()
+
+
+def wait_send(copies):
+    for copy in copies:
+        copy.wait_send()
+
+
+class Gather:
+    def __init__(self, links, full, shard, seg):
+        tensor, self.order, first, count = seg
+        self.links, self.full, self.shard = links, full, shard
+        self.blocked = tensor == 3
+        if self.blocked:
+            self.units = (pl.ds(first, count),)
+            self.all_cols = pl.ds(0, D)
+            width = D // 4
+            self.z_cols = pl.ds(pl.multiple_of(links.z * width, width), width)
+        else:
+            self.units = ()
+            self.all_cols = pl.ds(first * D, count * D)
+            width = count * D // 4
+            self.z_cols = pl.ds(pl.multiple_of(first * D + links.z * width, width), width)
+        self.sent = []
+
+    def view(self, x, yh, yl, cols):
+        return self.full.at[(x, yh, self.links.core) + self.units + (yl, NONE, cols)]
+
+    def own(self, cols):
+        return self.shard.at[self.units + (self.links.yl, NONE, cols)]
+
+    def push(self, src, dst, axis):
+        now = [self.links.to(src, dst, who) for who in self.links.peers(axis)]
+        self.sent += now
+        return now
+
+    def stage1(self):
+        k = self.links
+        cols = self.all_cols if self.order == 0 else self.z_cols
+        dst = self.view(k.x, k.yh, k.yl, cols)
+        self.kept = k.local(self.own(cols), dst)
+        self.first = self.push(self.own(cols), dst, "x" if self.order == 1 else "y")
+
+    def stage2(self):
+        k = self.links
+        self.kept.wait()
+        wait_recv(self.first)
+        if self.order == 0:
+            part = self.view(k.x, NONE, NONE, self.all_cols)
+            self.last = self.push(part, part, "x")
+        elif self.order == 1:
+            part = self.view(NONE, k.yh, k.yl, self.z_cols)
+            self.second = self.push(part, part, "z")
+        else:
+            part = self.view(k.x, NONE, NONE, self.z_cols)
+            self.second = self.push(part, part, "x")
+
+    def stage3(self):
+        k = self.links
+        if self.order == 0:
+            return
+        wait_recv(self.second)
+        if self.order == 1:
+            part = self.view(NONE, k.yh, k.yl, self.all_cols)
+            self.last = self.push(part, part, "y")
+        else:
+            part = self.view(NONE, NONE, NONE, self.z_cols)
+            self.last = self.push(part, part, "z")
+
+    def cross(self):
+        wait_recv(self.last)
+        part = self.view(NONE, NONE, NONE, self.all_cols)
+        self.swapped = self.push(part, part, "core")
+
+    def finish(self):
+        wait_recv(self.swapped)
+
+    def drain(self):
+        wait_send(self.sent)
+
+
+def small_row(pack, row):
+    pieces = []
+    for x in range(4):
+        for yh in range(2):
+            pieces.append(
+                pack[x, yh, 0, row : row + 1, :].astype(F32)
+                + pack[x, yh, 1, row : row + 1, :].astype(F32)
+            )
+    return jnp.concatenate(pieces, axis=1)
+
+
+def dot_nt(a, b):
+    return lax.dot_general(a, b, (((1,), (1,)), ((), ())), preferred_element_type=F32)
+
+
+def dot_tn(a, b):
+    return lax.dot_general(a, b, (((0,), (0,)), ((), ())), preferred_element_type=F32)
+
+
+def dot(a, b):
+    return jnp.dot(a, b, preferred_element_type=F32)
+
+
+def slope_of(links, h, shape):
+    power = (links.me * 2 + h + 1).astype(F32) * -0.5
+    return jnp.exp2(jnp.full(shape, power, F32)) * (4.0 / LENGTH)
+
+
+def extend(links, seg_ref, qkv_ref, kx_ref, qx_ref, h, t):
+    rows = pl.ds(t * BLK, BLK)
+    seg = jnp.broadcast_to(seg_ref[t, 0:1, :].astype(F32), (128, BLK)).T
+    lane = lax.broadcasted_iota(jnp.int32, (BLK, 128), 1)
+    mine = (lane // 64) == h
+    e = lane - 64 * (1 - h)
+    where = lax.broadcasted_iota(jnp.int32, (BLK, 128), 0) + t * BLK
+    bias = slope_of(links, h, (BLK, 128)) * where.astype(F32)
+    high = bias.astype(BF).astype(F32)
+    mid = (bias - high).astype(BF).astype(F32)
+    low = bias - high - mid
+    doc = (e - 3).astype(F32)
+    is_doc = (e >= 3) & (e <= 6)
+    same = seg == doc
+    key_extra = jnp.where(is_doc & jnp.logical_not(same), 1.0, 0.0)
+    key_extra = jnp.where(e == 0, high, jnp.where(e == 1, mid, jnp.where(e == 2, low, key_extra)))
+    query_extra = jnp.where(is_doc & same, -BIG, 0.0)
+    query_extra = jnp.where((e >= 0) & (e <= 2), 1.0, query_extra)
+    query = qkv_ref[0, rows, :].astype(F32) * 0.125
+    key = qkv_ref[1, rows, :].astype(F32)
+    kx_ref[h, rows, :] = jnp.where(mine, key, key_extra).astype(BF)
+    qx_ref[h, rows, :] = jnp.where(mine, query, query_extra).astype(BF)
+
+
+def attend(links, kx_ref, qx_ref, vt_ref, ot_ref, lse_ref, h, i):
+    keys = BLK * (i + 1)
+    qb = qx_ref[h, BLK * i : keys, :]
+    down = lax.broadcasted_iota(jnp.int32, (BLK, BLK), 0)
+    across = lax.broadcasted_iota(jnp.int32, (BLK, BLK), 1)
+    edge = jnp.where(down <= across, dot_nt(kx_ref[h, BLK * i : keys, :], qb), -BIG)
+    top = jnp.max(edge, axis=0, keepdims=True)
+    if i:
+        past = dot_nt(kx_ref[h, 0 : BLK * i, :], qb)
+        top = jnp.maximum(top, jnp.max(past, axis=0, keepdims=True))
+    edge = jnp.exp(edge - top)
+    total = jnp.sum(edge, axis=0, keepdims=True)
+    out = dot(vt_ref[h, :, BLK * i : keys], edge.astype(BF))
+    if i:
+        past = jnp.exp(past - top)
+        total = total + jnp.sum(past, axis=0, keepdims=True)
+        out = out + dot(vt_ref[h, :, 0 : BLK * i], past.astype(BF))
+    ot_ref[h, :, BLK * i : keys] = out / total
+    where = (lax.broadcasted_iota(jnp.int32, (1, BLK), 1) + BLK * i).astype(F32)
+    lse_ref[h, :, BLK * i : keys] = jnp.broadcast_to(
+        top + jnp.log(total) - slope_of(links, h, (1, BLK)) * where, (8, BLK)
+    )
+
+
+def forward_kernel(
+    tokens,
+    seg,
+    small,
+    wq_in,
+    wo_in,
+    w1_in,
+    w2_in,
+    wq_out,
+    wo,
+    w1,
+    w2,
+    pack_out,
+    normed_out,
+    qkv_out,
+    ot,
+    lse,
+    mixed,
+    lse_all,
+    wq,
+    pack,
+    seg_all,
+    row,
+    merged,
+    qkv,
+    kx,
+    qx,
+    vt,
+    mixed_send,
+    send,
+    recv,
+):
+    k = Links(send, recv)
+    k.barrier()
+    sent, kept = [], []
+
+    kept_small = k.local(small, pack.at[k.x, k.yh, k.core])
+    small_x = [k.to(small, pack.at[k.x, k.yh, k.core], who) for who in k.peers("x")]
+    fulls, shards = (wq, wo, w1, w2), (wq_in, wo_in, w1_in, w2_in)
+    first = [Gather(k, fulls[s[0]], shards[s[0]], s) for s in QKV_SEGS]
+    rest = [Gather(k, fulls[s[0]], shards[s[0]], s) for s in REST_SEGS]
+    for g in first:
+        g.stage1()
+    kept_seg = k.local(seg, seg_all.at[k.me])
+    segs = [k.to(seg, seg_all.at[k.me], who) for _, who in k.rows_peers()]
+    for g in first:
+        g.stage2()
+    kept_small.wait()
+    wait_recv(small_x)
+    part = pack.at[:, k.yh, k.core]
+    small_y = [k.to(part, part, k.peers("y")[1])]
+    for g in rest:
+        g.stage1()
+    for g in first:
+        g.stage3()
+    wait_recv(small_y)
+    part = pack.at[:, :, k.core]
+    small_c = [k.to(part, part, k.peers("core")[0])]
+
+    values = tokens[...].astype(F32)
+    center = values - jnp.mean(values, axis=1, keepdims=True)
+    center = center * lax.rsqrt(jnp.mean(center * center, axis=1, keepdims=True) + 1e-05)
+    wait_recv(small_c)
+    normed_out[...] = (center * small_row(pack, 0) + small_row(pack, 1)).astype(BF)
+    pack_out[...] = pack[...]
+    pieces = []
+    for f in range(16):
+        pieces.append(pack[f // 4, (f // 2) % 2, f % 2, 6:7, :].astype(F32))
+    row[...] = jnp.broadcast_to(
+        jnp.concatenate(pieces[:8] + [jnp.zeros((1, D), F32)] + pieces[8:], axis=1), (8, 3 * D)
+    )
+    for g in first:
+        g.cross()
+    for g in rest:
+        g.stage2()
+    for g in first:
+        g.finish()
+    kept.append(k.local(wq, wq_out))
+
+    @pl.loop(0, 12)
+    def _(n):
+        cols = pl.ds(pl.multiple_of(n * 256, 256), 256)
+        weight = wq[:, :, :, :, :, cols].reshape(D, 256)
+        block = (dot(normed_out[...], weight) + row[0:1, cols]).astype(BF)
+        merged[n // 4, 2 * (n % 4)] = block[:, :128]
+        merged[n // 4, 2 * (n % 4) + 1] = block[:, 128:]
+
+    mine = pl.ds(pl.multiple_of(k.me * BLK, BLK), BLK)
+    kept_qkv = k.local(merged.at[:, k.me], qkv.at[:, mine])
+    moved = [k.to(merged.at[:, t], qkv.at[:, mine], who) for t, who in k.rows_peers()]
+    for g in rest:
+        g.stage3()
+    kept_seg.wait()
+    wait_recv(segs)
+    kept_qkv.wait()
+    wait_recv(moved)
+    kept.append(k.local(qkv, qkv_out))
+
+    @pl.loop(0, 8)
+    def _(t):
+        for h in range(2):
+            extend(k, seg_all, qkv, kx, qx, h, t)
+
+    for t in range(8):
+        flipped = qkv[2, BLK * t : BLK * (t + 1), :].astype(F32).T.astype(BF)
+        for h in range(2):
+            vt[h, :, BLK * t : BLK * (t + 1)] = flipped[64 * h : 64 * (h + 1)]
+
+    for i in range(8):
+
+        @pl.loop(0, 2)
+        def _(h):
+            attend(k, kx, qx, vt, ot, lse, h, i)
+
+        both = jnp.concatenate(
+            [ot[0, :, BLK * i : BLK * (i + 1)], ot[1, :, BLK * i : BLK * (i + 1)]], axis=0
+        )
+        mixed_send[i] = both.T.astype(BF)
+
+    cols = pl.ds(pl.multiple_of(k.me * 128, 128), 128)
+    kept.append(k.local(mixed_send.at[k.me], mixed.at[:, cols]))
+    back = [k.to(mixed_send.at[t], mixed.at[:, cols], who) for t, who in k.rows_peers()]
+    part = pl.ds(pl.multiple_of(k.me * BLK, BLK), BLK)
+    kept.append(k.local(lse.at[:, :, part], lse_all.at[k.me]))
+    for t, who in k.rows_peers():
+        part = pl.ds(pl.multiple_of(t * BLK, BLK), BLK)
+        back.append(k.to(lse.at[:, :, part], lse_all.at[k.me], who))
+    for g in rest:
+        g.cross()
+    wait_recv(back)
+    for g in rest:
+        g.finish()
+    for copy in kept:
+        copy.wait()
+    for g in first + rest:
+        g.drain()
+    wait_send(small_x + small_y + small_c + segs + moved + back)
+
+
+def full_shape(cols):
+    return (4, 2, 2, 2, 32, cols)
+
+
+def forward_call(tokens, seg, small, wq, wo, w1, w2):
+    hbm = pl.BlockSpec(memory_space=pl.ANY)
+    vmem = pl.BlockSpec(memory_space=pltpu.VMEM)
+    out = jax.ShapeDtypeStruct
+    return pl.pallas_call(
+        forward_kernel,
+        name="forward",
+        out_shape=(
+            out(full_shape(3 * D), BF),
+            out(full_shape(D), BF),
+            out(full_shape(4 * D), BF),
+            out((4, 2, 2, 4, 2, 32, D), BF),
+            out((4, 2, 2, 16, 128), BF),
+            out((BLK, D), BF),
+            out((3, LENGTH, 128), BF),
+            out((2, 64, LENGTH), F32),
+            out((2, 8, LENGTH), F32),
+            out((BLK, D), BF),
+            out((8, 2, 8, BLK), F32),
+        ),
+        in_specs=[vmem, vmem, vmem, hbm, hbm, hbm, hbm],
+        out_specs=(hbm, hbm, hbm, hbm, vmem, vmem, hbm, vmem, vmem, hbm, hbm),
+        scratch_shapes=[
+            pltpu.VMEM(full_shape(3 * D), BF),
+            pltpu.VMEM((4, 2, 2, 16, 128), BF),
+            pltpu.VMEM((8, 8, BLK), jnp.int32),
+            pltpu.VMEM((8, 3 * D), F32),
+            pltpu.VMEM((3, 8, BLK, 128), BF),
+            pltpu.VMEM((3, LENGTH, 128), BF),
+            pltpu.VMEM((2, LENGTH, 128), BF),
+            pltpu.VMEM((2, LENGTH, 128), BF),
+            pltpu.VMEM((2, 64, LENGTH), BF),
+            pltpu.VMEM((8, BLK, 128), BF),
+            pltpu.SemaphoreType.DMA((170,)),
+            pltpu.SemaphoreType.DMA((170,)),
+        ],
+        compiler_params=pltpu.CompilerParams(
+            collective_id=0, has_side_effects=True, vmem_limit_bytes=50 * MIB
+        ),
+    )(
+        tokens,
+        seg,
+        small,
+        wq.reshape(2, 32, 3 * D),
+        wo.reshape(2, 32, D),
+        w1.reshape(2, 32, 4 * D),
+        w2.reshape(4, 2, 32, D),
+    )
+
+
+def small_pack(ln1_gain, ln1_bias, ln2_gain, ln2_bias, out_bias, fc2_bias, qkv_bias, fc1_bias):
+    core = lax.axis_index("fsdp") % 2
+    six = jnp.stack([ln1_gain, ln1_bias, ln2_gain, ln2_bias, out_bias, fc2_bias])
+    none = jnp.zeros_like(six)
+    halves = jnp.where(
+        core == 0, jnp.concatenate([six, none], 1), jnp.concatenate([none, six], 1)
+    )
+    return jnp.concatenate(
+        [halves, qkv_bias[None], fc1_bias.reshape(2, 128), jnp.zeros((7, 128), BF)], 0
+    )
+
+
+def unpack_row(pack, row):
+    return (pack[:, :, 0, row] + pack[:, :, 1, row]).reshape(D)
 
 
 def layer_norm(values, gain_vec, bias_vec):
@@ -79,97 +532,44 @@
     row_count, block_len, _ = tokens.shape
     flat_rows = row_count * block_len
     full_length = block_len * lax.axis_size("ctx")
-    forward_full = (
-        lax.all_gather(ln1_gain, "fsdp", axis=0, tiled=True),
-        lax.all_gather(ln1_bias, "fsdp", axis=0, tiled=True),
-        lax.all_gather(qkv_weight, "fsdp", axis=0, tiled=True),
-        lax.all_gather(qkv_bias, "fsdp", axis=0, tiled=True),
-        lax.all_gather(out_weight, "fsdp", axis=0, tiled=True),
-        lax.all_gather(out_bias, "fsdp", axis=0, tiled=True),
-        lax.all_gather(ln2_gain, "fsdp", axis=0, tiled=True),
-        lax.all_gather(ln2_bias, "fsdp", axis=0, tiled=True),
-        lax.all_gather(fc1_weight, "fsdp", axis=0, tiled=True),
-        lax.all_gather(fc1_bias, "fsdp", axis=0, tiled=True),
-        lax.all_gather(fc2_weight, "fsdp", axis=0, tiled=True),
-        lax.all_gather(fc2_bias, "fsdp", axis=0, tiled=True),
-    )
-    (
-        gain_one,
-        bias_one,
-        qkv_mat,
-        qkv_vec,
-        out_mat,
-        out_vec,
-        gain_two,
-        bias_two,
-        up_mat,
-        up_vec,
-        down_mat,
-        down_vec,
-    ) = forward_full
-    gain_one_f = gain_one.astype(jnp.float32)
-    bias_one_f = bias_one.astype(jnp.float32)
-    gain_two_f = gain_two.astype(jnp.float32)
-    bias_two_f = bias_two.astype(jnp.float32)
+    small = small_pack(
+        ln1_gain, ln1_bias, ln2_gain, ln2_bias, out_bias, fc2_bias, qkv_bias, fc1_bias
+    )
+    (qkv_mat, out_mat, up_mat, down_mat, pack, normed, qkv_heads, mixed_heads, lse_heads, mixed, lse_all) = forward_call(
+        tokens.reshape(flat_rows, D),
+        jnp.broadcast_to(segment_ids, (8, block_len)),
+        small,
+        qkv_weight,
+        out_weight,
+        fc1_weight,
+        fc2_weight,
+    )
+    qkv_mat = qkv_mat.reshape(D, 3 * D)
+    out_mat = out_mat.reshape(D, D)
+    up_mat = up_mat.reshape(D, 4 * D)
+    down_mat = down_mat.reshape(4 * D, D)
+    gain_one_f = unpack_row(pack, 0).astype(jnp.float32)
+    bias_one_f = unpack_row(pack, 1).astype(jnp.float32)
+    gain_two_f = unpack_row(pack, 2).astype(jnp.float32)
+    bias_two_f = unpack_row(pack, 3).astype(jnp.float32)
+    out_vec = unpack_row(pack, 4)
+    down_vec = unpack_row(pack, 5)
+    qkv_vec = pack[:, :, :, 6].reshape(2 * D)
+    up_vec = pack[:, :, :, 7:9].reshape(4 * D)
     inputs = tokens.astype(jnp.float32).reshape(flat_rows, D)
-    normed = layer_norm(inputs, gain_one_f, bias_one_f).astype(jnp.bfloat16)
-    qkv_float = qkv_vec.astype(jnp.float32)
-    merged_bias = jnp.concatenate([qkv_float[:D], jnp.zeros((D,), jnp.float32), qkv_float[D:]])
+    merged_bias = jnp.concatenate([qkv_vec[:D], jnp.zeros((D,), BF), qkv_vec[D:]]).astype(jnp.float32)
     merged = (matmul(normed, qkv_mat) + merged_bias).astype(jnp.bfloat16)
     query = merged[:, :D].reshape(row_count, block_len, HEADS, HEAD_DIM)
     key_values = merged[:, D:].reshape(row_count, block_len, 2 * D)
     query_pos = lax.axis_index("ctx") * block_len + jnp.arange(block_len, dtype=jnp.int32)
-    first_row = jnp.int32(0)
-    running_top = jnp.full((row_count, HEADS, block_len), -1e30, jnp.float32)
-    running_sum = jnp.zeros((row_count, HEADS, block_len), jnp.float32)
-    weighted = jnp.zeros((row_count, block_len, HEADS, HEAD_DIM), jnp.float32)
-    key_rows = lax.all_gather(key_values, "ctx", axis=1, tiled=True)
-    key_seg = lax.all_gather(segment_ids, "ctx", axis=1, tiled=True)
-    for offset, width_now in key_spans(key_rows.shape[1]):
-        scores, allowed, key_part, value_part = block_scores(
-            query,
-            segment_ids,
-            query_pos,
-            key_rows[:, offset : offset + width_now],
-            key_seg[:, offset : offset + width_now],
-            first_row + offset,
-        )
-        masked = jnp.where(allowed, scores, -1e30)
-        new_top = jnp.maximum(running_top, jnp.max(masked, axis=-1))
-        fade_out = jnp.exp(running_top - new_top)
-        expo = jnp.where(allowed, jnp.exp(scores - new_top[..., None]), 0.0)
-        running_sum = running_sum * fade_out + jnp.sum(expo, axis=-1)
-        weighted = weighted * jnp.swapaxes(fade_out, 1, 2)[..., None] + jnp.einsum(
-            "rhij,rjhd->rihd",
-            expo.astype(jnp.bfloat16),
-            value_part,
-            preferred_element_type=jnp.float32,
-        )
-        running_top = new_top
-    final_top, final_sum, weighted = (running_top, running_sum, weighted)
-    log_sums = final_top + jnp.log(final_sum)
-    mixed_exact = weighted / jnp.swapaxes(final_sum, 1, 2)[..., None]
-    mixed = mixed_exact.astype(jnp.bfloat16).reshape(flat_rows, D)
+    log_sums = lse_all[:, :, 0].reshape(1, HEADS, block_len)
+    mixed_exact = mixed.astype(jnp.float32).reshape(row_count, block_len, HEADS, HEAD_DIM)
     middle = inputs + matmul(mixed, out_mat) + out_vec.astype(jnp.float32)
     normed_two = layer_norm(middle, gain_two_f, bias_two_f).astype(jnp.bfloat16)
     hidden = matmul(normed_two, up_mat) + up_vec.astype(jnp.float32)
     active = gelu_tanh(hidden).astype(jnp.bfloat16)
     output = middle + matmul(active, down_mat) + down_vec.astype(jnp.float32)
-    back_full = (
-        lax.all_gather(ln1_gain, "fsdp", axis=0, tiled=True),
-        lax.all_gather(ln1_bias, "fsdp", axis=0, tiled=True),
-        lax.all_gather(qkv_weight, "fsdp", axis=0, tiled=True),
-        lax.all_gather(qkv_bias, "fsdp", axis=0, tiled=True),
-        lax.all_gather(out_weight, "fsdp", axis=0, tiled=True),
-        lax.all_gather(out_bias, "fsdp", axis=0, tiled=True),
-        lax.all_gather(ln2_gain, "fsdp", axis=0, tiled=True),
-        lax.all_gather(ln2_bias, "fsdp", axis=0, tiled=True),
-        lax.all_gather(fc1_weight, "fsdp", axis=0, tiled=True),
-        lax.all_gather(fc1_bias, "fsdp", axis=0, tiled=True),
-        lax.all_gather(fc2_weight, "fsdp", axis=0, tiled=True),
-        lax.all_gather(fc2_bias, "fsdp", axis=0, tiled=True),
-    )
-    _, _, qkv_back, _, out_back, _, _, _, up_back, _, down_back, _ = back_full
+    qkv_back, out_back, up_back, down_back = qkv_mat, out_mat, up_mat, down_mat
     grad_down = cotangent.reshape(flat_rows, D)
     grad_output = grad_down.astype(jnp.float32)
     fc2_weight_grad = matmul_tn(active, grad_down)

time: 1080 us -> 941 us (0.87)
  waiting for transfers between devices: 592 us -> 456 us
  Pallas kernels: 0 us -> 135 us
  blocking collectives: 216 us -> 101 us
  matrix products: 141 us -> 113 us
  other arithmetic: 70.7 us -> 56.2 us
  local copies, waits for them, and re-layouts: 40.5 us -> 52.6 us
    pallas_call x0 -> x1, Pallas kernels: none -> 135 us  [forward_call(): pl.pallas_call(forward_kernel, name='forward', out_shape=(out(full_shape(...]
    all_gather x4 -> x0, waiting for transfers between devices: 123 us -> none  [the longest x1 64.9 us: local(): lax.all_gather(fc2_weight, 'fsdp', axis=0, tiled=True)]
    unnamed x2 -> x1, blocking collectives: 136 us -> 66 us
    all_gather x2 -> x0, blocking collectives: 41.4 us -> none  [the longest x1 22.3 us: local(): lax.all_gather(fc1_bias, 'fsdp', axis=0, tiled=True)]
    reduce_sum x2 -> x0, other arithmetic: 12.4 us -> none  [local(): running_sum = running_sum * fade_out + jnp.sum(expo, axis=-1)]
  transfers between devices with their start and end apart: 11 -> 7, of which waited for: 8 -> 6; matrix products, arithmetic and copies ran while one was open for 13% -> 10% of each run, Pallas kernels for 0% -> 0%
where the time goes in v1:
time: 941 us; the launch traced here: 932 us
  waiting for transfers between devices  456 us (48%)
  Pallas kernels  135 us (14%)
  matrix products  113 us (12%)
  blocking collectives  101 us (11%)
  other arithmetic  56.2 us (6%)
  local copies, waits for them, and re-layouts  52.6 us (6%)
  between operations  17.3 us (2%)
    pallas_call x1, Pallas kernels, forward_call(): pl.pallas_call(forward_kernel, name='forward', out_shape=(out(full_shape(...  135 us
    reduce_scatter x1, waiting for transfers between devices, local(): lax.psum_scatter(fc2_weight_grad.astype(jnp.bfloat16), 'fsdp', scatter_di...  106 us
    reduce_scatter x1, waiting for transfers between devices, local(): lax.psum_scatter(fc1_weight_grad.astype(jnp.bfloat16), 'fsdp', scatter_di...  105 us
    reduce_scatter x1, waiting for transfers between devices, local(): lax.psum_scatter(qkv_weight_grad.astype(jnp.bfloat16), 'fsdp', scatter_di...  92.4 us
    unnamed x1, blocking collectives  66 us
    reduce_scatter x1, waiting for transfers between devices, local(): lax.psum_scatter(grad_keys.astype(jnp.bfloat16), 'ctx', scatter_dimension...  60.8 us
    reduce_scatter x1, waiting for transfers between devices, local(): lax.psum_scatter(out_weight_grad.astype(jnp.bfloat16), 'fsdp', scatter_di...  54.1 us
    all_gather x1, waiting for transfers between devices, local(): key_rows = lax.all_gather(key_values, 'ctx', axis=1, tiled=True)  37.4 us
  transfers between devices with their start and end apart: 7, of which 6 were waited for; matrix products, arithmetic and copies ran while one was open for 10% of the time, Pallas kernels for 0%

profile of v1, /device:TPU:0, one launch (start us, length us, event | category | flops | bytes accessed | tf_op | source)
XLA Modules:
  0.0 931.8 jit_solution(13630367289222890663)
XLA Ops:
  14.6 135.0 %forward.1 = (bf16[4,2,2,2,32,3072]{5,4,3,2,1,0:T(8,128)(2,1)}, bf16[4,2,2,2,32,1024]{5,4,3,2,1,0:T(8,128)(2,1)}, bf16[4,2,2,2,32,4096]{5,4,3,2,1,0:T(8,128)(2,1...) custom-call(bf16[256,1024]{1,0:T(8,128)(2,1)S(1)} %bitcast.195, ...), custom_call_target="tpu_custom_call" | custom-call | tf_op jit(solution)/shard_map/forward/pallas_call | solution.py:403
  149.6 4.6 fusion.25
  162.6 6.1 convolution_add_fusion
  168.8 5.4 fusion.74
  187.0 15.5 %all_gather.7 = s32[1,2048]{1,0:T(1,128)S(1)} all-gather(s32[1,256]{1,0:T(1,128)S(1)} %copy-done.50), channel_id=1, replica_groups=mesh['ctx'=8,'fsdp'=16] {'ctx'}, dimensions={1}, use_global_device_ids=true | all-gather | bytes 9216 | tf_op jit(solution)/shard_map/all_gather | solution.py:599
  208.5 37.4 %all-gather.3.cloned.1.call-done = bf16[2048,2048]{1,0:T(8,128)(2,1)} async-done(((bf16[256,2048]{1,0:T(8,128)(2,1)}), bf16[2048,2048]{1,0:T(8,128)(2,1)}) %all-gather.3.cloned.1.call-update) | async-done | bytes 8388624 | tf_op jit(solution)/shard_map/all_gather | solution.py:598
  245.9 6.0 fusion.69
  272.9 3.6 fusion.19
  276.5 4.0 multiply_convert_fusion.3
  283.9 3.6 fusion.17
  287.5 4.1 multiply_convert_fusion.2
  294.9 3.9 fusion.15
  298.8 4.1 multiply_convert_fusion.1
  309.9 4.0 multiply_convert_fusion
  316.5 7.6 select_maximum_fusion
  324.1 4.3 maximum_dynamic-update-slice_fusion
  328.4 5.3 fusion.12
  333.7 5.2 fusion.11
  338.9 9.1 convert_element_type.301
  351.5 8.5 convolution_convert_fusion
  360.1 7.3 convolution_convert_fusion.1
  368.6 3.8 fusion.76
  378.8 60.8 %reduce-scatter.6.cloned.1.call-done = bf16[1,256,2048]{1,2,0:T(8,128)(2,1)} async-done(((bf16[1,2048,2048]{1,2,0:T(8,128)(2,1)}), bf16[1,256,2048]{1,2,0:T(8,128)(2,1)}) %reduce-scatter.6.cloned.1.call-update) | async-done | bytes 1048592 | tf_op jit(solution)/shard_map/reduce_scatter | solution.py:637
  439.6 5.8 convolution_convert_fusion.2
  449.9 8.6 fusion.36
  459.0 54.1 %reduce-scatter.10.cloned.1.call-done = bf16[64,1024]{1,0:T(8,128)(2,1)} async-done(((bf16[1024,1024]{1,0:T(8,128)(2,1)}), bf16[64,1024]{1,0:T(8,128)(2,1)}) %reduce-scatter.10.cloned.1.call-update) | async-done | bytes 131088 | tf_op jit(solution)/shard_map/reduce_scatter | solution.py:663
  513.1 105.9 %reduce-scatter.14.cloned.1.call-done = bf16[256,1024]{1,0:T(8,128)(2,1)} async-done(((bf16[4096,1024]{1,0:T(8,128)(2,1)}), bf16[256,1024]{1,0:T(8,128)(2,1)}) %reduce-scatter.14.cloned.1.call-update) | async-done | bytes 524304 | tf_op jit(solution)/shard_map/reduce_scatter | solution.py:681
  619.0 105.5 %reduce-scatter.12.cloned.1.call-done = bf16[64,4096]{1,0:T(8,128)(2,1)} async-done(((bf16[1024,4096]{1,0:T(8,128)(2,1)}), bf16[64,4096]{1,0:T(8,128)(2,1)}) %reduce-scatter.12.cloned.1.call-update) | async-done | bytes 524304 | tf_op jit(solution)/shard_map/reduce_scatter | solution.py:675
  724.5 92.4 %reduce-scatter.8.cloned.1.call-done = bf16[64,3072]{1,0:T(8,128)(2,1)} async-done(((bf16[1024,3072]{1,0:T(8,128)(2,1)}), bf16[64,3072]{1,0:T(8,128)(2,1)}) %reduce-scatter.8.cloned.1.call-update) | async-done | bytes 393232 | tf_op jit(solution)/shard_map/reduce_scatter | solution.py:657
  816.9 5.2 fusion.65
  823.8 66.0 %all-reduce.11 = (bf16[1024]{0:T(1024)(128)(2,1)S(1)}, bf16[1024]{0:T(1024)(128)(2,1)S(1)}, bf16[2048]{0:T(1024)(128)(2,1)S(1)}, bf16[1024]{0:T(1024)(128)(2,1)S...) all-reduce(bf16[1024]{0:T(1024)(128)(2,1)S(1)} %get-tuple-element.7, ...), channel_id=4, replica_groups=mesh['ctx'=8,'fsdp'=16] {'fsdp'}, use_global_device_ids=true, to_apply=%region_11.12.clone | all-reduce | flops 12288 | bytes 49152
  890.4 19.5 %all-reduce.12 = (bf16[64]{0:T(256)(128)(2,1)S(1)}, bf16[64]{0:T(256)(128)(2,1)S(1)}, bf16[128]{0:T(256)(128)(2,1)S(1)}, bf16[64]{0:T(256)(128)(2,1)S(1)}, bf16[...) all-reduce(bf16[64]{0:T(256)(128)(2,1)S(1)} %dynamic-slice.1, ...), channel_id=1, replica_groups=mesh['ctx'=8,'fsdp'=16] {'ctx'}, use_global_device_ids=true, to_apply=%region_12.13 | all-reduce | flops 768 | bytes 3072 | tf_op jit(solution)/shard_map/psum | solution.py:689
  (233 shorter events, 102.3 us)
Async XLA Ops:
  7.2 238.7 %all-gather.3.cloned.1.call-start = ((), (), s32[]{:S(2)}) async-start(), calls=%async_computation.10 | async-start | bytes 9437184 | tf_op jit(solution)/shard_map/all_gather | solution.py:598
  155.4 4.6 copy-start.1
  156.4 283.2 %reduce-scatter.6.cloned.1.call-start = ((), (), s32[]{:S(2)}) async-start(), calls=%async_computation.5 | async-start | bytes 9437184 | tf_op jit(solution)/shard_map/reduce_scatter | solution.py:637
  162.3 6.5 slice-start
  162.6 6.2 copy-start.23
  162.6 6.2 slice-start.1
  162.6 11.6 %slice-start.2 = ((s8[8388608]{0:T(1024)(128)(4,1)}), s8[4194304]{0:T(1024)(128)(4,1)S(1)}, s32[]{:S(2)}) async-start(s8[8388608]{0:T(1024)(128)(4,1)} %bitcast.283), calls=%async_computation.14 | async-start | bytes 8388608
  168.8 5.5 copy-start.58
  168.8 5.4 slice-start.3
  177.9 7.1 copy-start.48
  179.6 7.4 copy-start.50
  294.9 3.9 copy-start.35
  324.1 4.3 copy-start.31
  328.4 5.3 copy-start.22
  328.4 5.3 copy-start.32
  348.0 165.1 %reduce-scatter.10.cloned.1.call-start = ((), (), s32[]{:S(2)}) async-start(), calls=%async_computation.7 | async-start | bytes 2228224 | tf_op jit(solution)/shard_map/reduce_scatter | solution.py:663
  351.2 267.7 %reduce-scatter.14.cloned.1.call-start = ((), (), s32[]{:S(2)}) async-start(), calls=%async_computation.9 | async-start | bytes 8912896 | tf_op jit(solution)/shard_map/reduce_scatter | solution.py:681
  360.0 364.4 %reduce-scatter.12.cloned.1.call-start = ((), (), s32[]{:S(2)}) async-start(), calls=%async_computation.8 | async-start | bytes 8912896 | tf_op jit(solution)/shard_map/reduce_scatter | solution.py:675
  367.4 449.4 %reduce-scatter.8.cloned.1.call-start = ((), (), s32[]{:S(2)}) async-start(), calls=%async_computation.6 | async-start | bytes 6684672 | tf_op jit(solution)/shard_map/reduce_scatter | solution.py:657
  368.6 3.8 copy-start.8
  368.6 3.8 copy-start.18
  445.4 3.7 copy-start.44
  445.4 4.5 copy-start.53
  445.5 471.3 %all-reduce.16.cloned.1.call-start = ((), (), s32[]{:S(2)}) async-start(), calls=%async_computation.11 | async-start | bytes 3145728 | tf_op jit(solution)/shard_map/psum | solution.py:691
  449.9 8.6 copy-start.27
  449.9 367.0 %copy-start.45 = (f32[4,2,1,1,128]{4,3,2,1,0:T(1,128)S(1)}, f32[4,2,1,1,128]{4,3,2,1,0:T(1,128)}, u32[]{:S(2)}) copy-start(f32[4,2,1,1,128]{4,3,2,1,0:T(1,128)} %get-tuple-element.120) | copy-start | bytes 12292
  816.9 6.8 copy-start.51
  816.9 6.8 copy-start.52
  816.9 6.8 copy-start.54
  816.9 6.8 copy-start.55
  816.9 97.1 %copy-start.14 = (f32[256,1024]{1,0:T(8,128)S(1)}, f32[256,1024]{1,0:T(8,128)}, u32[]{:S(2)}) copy-start(f32[256,1024]{1,0:T(8,128)} %copy-done.13) | copy-start | bytes 3145732
  816.9 97.1 %copy-start.49 = (f32[256]{0:T(256)S(1)}, f32[256]{0:T(256)}, u32[]{:S(2)}) copy-start(f32[256]{0:T(256)} %copy-done.48) | copy-start | bytes 3076
  (38 other events, 81.8 us)
Sparse Core Ops, SparseCore 0:
  156.6 89.2 all-gather.2
  348.1 91.4 reduce-scatter.5
  443.6 69.4 reduce-scatter.9
  517.3 101.6 reduce-scatter.13
  623.1 101.2 reduce-scatter.11
  728.5 88.3 reduce-scatter.7
  819.6 79.1 all-reduce.15

commit v2 on v1

--- a/solution.py
+++ b/solution.py
@@ -248,9 +248,10 @@
         out = out + dot(vt_ref[h, :, 0 : BLK * i], past.astype(BF))
     ot_ref[h, :, BLK * i : keys] = out / total
     where = (lax.broadcasted_iota(jnp.int32, (1, BLK), 1) + BLK * i).astype(F32)
-    lse_ref[h, :, BLK * i : keys] = jnp.broadcast_to(
-        top + jnp.log(total) - slope_of(links, h, (1, BLK)) * where, (8, BLK)
-    )
+    shifted = top + jnp.log(total)
+    final = shifted - slope_of(links, h, (1, BLK)) * where
+    first = lax.broadcasted_iota(jnp.int32, (8, BLK), 0) == 0
+    lse_ref[h, :, BLK * i : keys] = jnp.where(first, final, shifted)
 
 
 def forward_kernel(
@@ -268,6 +269,8 @@
     pack_out,
     normed_out,
     qkv_out,
+    kx,
+    qx,
     ot,
     lse,
     mixed,
@@ -278,8 +281,6 @@
     row,
     merged,
     qkv,
-    kx,
-    qx,
     vt,
     mixed_send,
     send,
@@ -411,13 +412,15 @@
             out((4, 2, 2, 16, 128), BF),
             out((BLK, D), BF),
             out((3, LENGTH, 128), BF),
+            out((2, LENGTH, 128), BF),
+            out((2, LENGTH, 128), BF),
             out((2, 64, LENGTH), F32),
             out((2, 8, LENGTH), F32),
             out((BLK, D), BF),
             out((8, 2, 8, BLK), F32),
         ),
         in_specs=[vmem, vmem, vmem, hbm, hbm, hbm, hbm],
-        out_specs=(hbm, hbm, hbm, hbm, vmem, vmem, hbm, vmem, vmem, hbm, hbm),
+        out_specs=(hbm, hbm, hbm, hbm, vmem, vmem, hbm, vmem, vmem, vmem, vmem, hbm, hbm),
         scratch_shapes=[
             pltpu.VMEM(full_shape(3 * D), BF),
             pltpu.VMEM((4, 2, 2, 16, 128), BF),
@@ -425,8 +428,6 @@
             pltpu.VMEM((8, 3 * D), F32),
             pltpu.VMEM((3, 8, BLK, 128), BF),
             pltpu.VMEM((3, LENGTH, 128), BF),
-            pltpu.VMEM((2, LENGTH, 128), BF),
-            pltpu.VMEM((2, LENGTH, 128), BF),
             pltpu.VMEM((2, 64, LENGTH), BF),
             pltpu.VMEM((8, BLK, 128), BF),
             pltpu.SemaphoreType.DMA((170,)),
@@ -462,6 +463,495 @@
     return (pack[:, :, 0, row] + pack[:, :, 1, row]).reshape(D)
 
 
+REST_UNITS = (
+    (3, 0, 0),
+    (3, 1, 1),
+    (3, 2, 2),
+    (3, 3, 2),
+    (2, 0, 0),
+    (2, 1, 0),
+    (2, 2, 1),
+    (2, 3, 2),
+    (1, 0, 0),
+)
+QKV_UNITS = ((0, 0, 0), (0, 1, 1), (0, 2, 2))
+UNITS = REST_UNITS + QKV_UNITS
+R1 = ((3, 2, 2, 32, D), (3, 4, 32, D), (3, 4, 2, 2, 32, 256))
+R2 = ((3, 32, D), (3, 4, 32, 256), (3, 2, 2, 32, 256))
+
+
+def count_of(order):
+    return sum(1 for unit in UNITS if unit[2] == order)
+
+
+class Reduce:
+    def __init__(self, links, unit, n, grads, half, slots):
+        self.tensor, self.unit, self.order = unit
+        self.links, self.grad = links, grads[self.tensor]
+        self.half = half.at[n]
+        at = sum(1 for other in UNITS[:n] if other[2] == self.order)
+        self.r1 = slots[self.order].at[at]
+        self.r2 = slots[3 + self.order].at[at]
+        self.r3 = slots[6].at[n]
+        self.z_cols = self.cols_of(links.z)
+        self.sent = []
+
+    def cols_of(self, z):
+        return pl.ds(pl.multiple_of(z * 256, 256), 256)
+
+    def of_core(self, core):
+        if self.tensor == 3:
+            return self.grad.at[:, :, core, self.unit]
+        return self.grad.at[:, :, core, :, :, pl.ds(self.unit * D, D)]
+
+    def stage0(self):
+        k = self.links
+        self.swap = k.to(self.of_core(1 - k.core), self.half, k.peers("core")[0])
+        self.sent.append(self.swap)
+
+    def push(self, axis, src_of, slot):
+        k = self.links
+        here = {"x": k.x, "y": k.y, "z": k.z}[axis]
+        self.coming = []
+        for j, who in enumerate(k.peers(axis)):
+            copy = k.to(src_of((here + j + 1) % 4), slot.at[j], who)
+            self.coming.append(copy)
+        self.sent += self.coming
+
+    def add0(self, own):
+        self.swap.wait_recv()
+
+        @pl.loop(0, 16)
+        def _(i):
+            x, yh, yl = i // 4, (i // 2) % 2, i % 2
+            total = self.half[x, yh, yl].astype(F32) + own(x, yh, yl).astype(F32)
+            self.half[x, yh, yl] = total.astype(BF)
+
+    def stage1(self):
+        half = self.half
+        if self.order == 0:
+            self.push("x", lambda x: half.at[x], self.r1)
+        elif self.order == 1:
+            self.push("y", lambda y: half.at[:, y // 2, y % 2], self.r1)
+        else:
+            self.push("z", lambda z: half.at[:, :, :, :, self.cols_of(z)], self.r1)
+
+    def sum1(self):
+        k, half, got = self.links, self.half, self.r1
+        wait_recv(self.coming)
+
+        @pl.loop(0, 16 if self.order == 2 else 4)
+        def _(i):
+            if self.order == 0:
+                spot, index = (k.x, i // 2, i % 2), (i // 2, i % 2)
+            elif self.order == 1:
+                spot, index = (i, k.yh, k.yl), (i,)
+            else:
+                index = (i // 4, (i // 2) % 2, i % 2)
+                spot = index + (NONE, self.z_cols)
+            total = half[spot].astype(F32)
+            for j in range(3):
+                total = total + got[(j,) + index].astype(F32)
+            half[spot] = total.astype(BF)
+
+    def stage2(self):
+        k, half = self.links, self.half
+        if self.order == 0:
+            self.push("y", lambda y: half.at[k.x, y // 2, y % 2], self.r2)
+        elif self.order == 1:
+            self.push("z", lambda z: half.at[:, k.yh, k.yl, :, self.cols_of(z)], self.r2)
+        else:
+            self.push("x", lambda x: half.at[x, :, :, :, self.z_cols], self.r2)
+
+    def sum2(self):
+        k, half, got = self.links, self.half, self.r2
+        wait_recv(self.coming)
+        if self.order == 0:
+            spot = (k.x, k.yh, k.yl)
+            total = half[spot].astype(F32)
+            for j in range(3):
+                total = total + got[j].astype(F32)
+            half[spot] = total.astype(BF)
+            return
+
+        @pl.loop(0, 4)
+        def _(i):
+            if self.order == 1:
+                spot, index = (i, k.yh, k.yl, NONE, self.z_cols), (i,)
+            else:
+                spot, index = (k.x, i // 2, i % 2, NONE, self.z_cols), (i // 2, i % 2)
+            total = half[spot].astype(F32)
+            for j in range(3):
+                total = total + got[(j,) + index].astype(F32)
+            half[spot] = total.astype(BF)
+
+    def stage3(self):
+        k, half = self.links, self.half
+        if self.order == 0:
+            self.push("z", lambda z: half.at[k.x, k.yh, k.yl, :, self.cols_of(z)], self.r3)
+        elif self.order == 1:
+            self.push("x", lambda x: half.at[x, k.yh, k.yl, :, self.z_cols], self.r3)
+        else:
+            self.push("y", lambda y: half.at[k.x, y // 2, y % 2, :, self.z_cols], self.r3)
+
+    def sum3(self, out_ref, position):
+        k = self.links
+        wait_recv(self.coming)
+        total = self.half[k.x, k.yh, k.yl, :, self.z_cols].astype(F32)
+        for j in range(3):
+            total = total + self.r3[j].astype(F32)
+        out_ref[k.me, :, 256 * position : 256 * (position + 1)] = total.astype(BF)
+
+    def drain(self):
+        wait_send(self.sent)
+
+    def write(self, got, position, outs):
+        out = outs[self.tensor]
+        for t in range(8):
+            piece = got[t, :, 256 * position : 256 * (position + 1)].astype(F32)
+            if self.tensor == 3:
+                out[self.unit, t // 4, :, 256 * (t % 4) : 256 * (t % 4 + 1)] = piece
+            else:
+                first = self.unit * D + 256 * (t % 4)
+                out[t // 4, :, first : first + 256] = piece
+
+
+def attend_back(kx, qx, vx, kt, do, delta, lse, dqt, h, j):
+    keys = slice(BLK * j, BLK * (j + 1))
+    down = lax.broadcasted_iota(jnp.int32, (BLK, BLK), 0)
+    across = lax.broadcasted_iota(jnp.int32, (BLK, BLK), 1)
+    grad_key = grad_value = None
+    cuts = [BLK * j, BLK * (j + 1)] + list(range(BLK * (j + 1) + 768, LENGTH, 768))
+    if cuts[-1] < LENGTH:
+        cuts.append(LENGTH)
+    for n in range(len(cuts) - 1):
+        rows = slice(cuts[n], cuts[n + 1])
+        queries = qx[h, rows, :]
+        scores = dot_nt(kx[h, keys, :], queries)
+        if n == 0:
+            scores = jnp.where(down <= across, scores, -BIG)
+        probs = jnp.exp(scores - lse[h, 1:2, rows])
+        grad_out = do[rows, :]
+        grad_probs = dot_nt(vx[h, keys, :], grad_out)
+        grad_scores = (probs * (grad_probs - delta[h, 0:1, rows])).astype(BF)
+        value_part = dot(probs.astype(BF), grad_out)
+        key_part = dot(grad_scores, queries)
+        grad_value = value_part if n == 0 else grad_value + value_part
+        grad_key = key_part if n == 0 else grad_key + key_part
+        query_part = dot(kt[h, :, keys], grad_scores)
+        if j == 0:
+            dqt[h, :, rows] = query_part
+        else:
+            dqt[h, :, rows] += query_part
+    return grad_key, grad_value
+
+
+def backward_kernel(
+    g_out,
+    g_fc1,
+    g_fc2,
+    grad_mixed,
+    qkv,
+    kx,
+    qx,
+    ot,
+    lse,
+    normed,
+    wq_in,
+    pack,
+    tokens,
+    grad_middle,
+    small_in,
+    o_qkv,
+    o_out,
+    o_fc1,
+    o_fc2,
+    o_small,
+    input_grad,
+    half,
+    r1x,
+    r1y,
+    r1z,
+    r2x,
+    r2y,
+    r2z,
+    r3,
+    own,
+    g_qkv,
+    w_slot,
+    vx,
+    kt,
+    do,
+    delta,
+    dqt,
+    g_send,
+    g_merged,
+    normed_t,
+    f_rest,
+    f_qkv,
+    small,
+    small_core,
+    small_x,
+    small_y,
+    small_z,
+    gn,
+    send,
+    recv,
+):
+    k = Links(send, recv)
+    k.barrier()
+    grads = (g_qkv, g_out, g_fc1, g_fc2)
+    slots = (r1x, r1y, r1z, r2x, r2y, r2z, r3)
+    units = [Reduce(k, unit, n, grads, half, slots) for n, unit in enumerate(UNITS)]
+    rest, last = units[:9], units[9:]
+    for u in rest:
+        u.stage0()
+    mine = pl.ds(pl.multiple_of(k.me * BLK, BLK), BLK)
+
+    def heads_of(t):
+        return pl.ds(pl.multiple_of(t * 128, 128), 128)
+
+    kept_do = k.local(grad_mixed.at[:, heads_of(k.me)], do.at[mine])
+    moved = [
+        k.to(grad_mixed.at[:, heads_of(t)], do.at[mine], who) for t, who in k.rows_peers()
+    ]
+    loads = [k.local(u.of_core(k.core), own.at[n]) for n, u in enumerate(rest[:2])]
+
+    lane = lax.broadcasted_iota(jnp.int32, (BLK, 128), 1)
+    for t in range(8):
+        rows = slice(BLK * t, BLK * (t + 1))
+        value = qkv[2, rows, :]
+        flipped = qkv[1, rows, :].astype(F32).T.astype(BF)
+        for h in range(2):
+            vx[h, rows, :] = jnp.where((lane // 64) == h, value.astype(F32), 0.0).astype(BF)
+            kt[h, :, rows] = flipped[64 * h : 64 * (h + 1)]
+    normed_t[...] = normed[...].astype(F32).T.astype(BF)
+    kept_do.wait()
+    wait_recv(moved)
+    for t in range(8):
+        rows = slice(BLK * t, BLK * (t + 1))
+        flipped = do[rows, :].astype(F32).T
+        for h in range(2):
+            product = flipped[64 * h : 64 * (h + 1)] * ot[h, :, rows]
+            delta[h, :, rows] = jnp.broadcast_to(
+                jnp.sum(product, axis=0, keepdims=True), (8, BLK)
+            )
+    for n, u in enumerate(rest):
+        loads[n].wait()
+        u.add0(lambda x, yh, yl, n=n: own[n % 2, x, yh, yl])
+        u.stage1()
+        if n + 2 < len(rest):
+            loads.append(k.local(rest[n + 2].of_core(k.core), own.at[n % 2]))
+
+    back = []
+    for t, who in k.rows_peers():
+        i = k.used
+        k.used += 1
+        copy = pltpu.make_async_remote_copy(
+            src_ref=g_send.at[:, t],
+            dst_ref=g_merged.at[:, :, heads_of(k.me)],
+            send_sem=k.send.at[i],
+            recv_sem=k.recv.at[i],
+            device_id=who,
+        )
+        back.append((t, copy))
+    for j in range(8):
+        found = [attend_back(kx, qx, vx, kt, do, delta, lse, dqt, h, j) for h in range(2)]
+        left = (lane // 64) == 0
+        for s, position in ((1, 0), (2, 1)):
+            both = jnp.where(left, found[0][position], found[1][position])
+            g_send[s, j] = both.astype(BF)
+        rows = slice(BLK * j, BLK * (j + 1))
+        query = jnp.concatenate([dqt[0, :, rows], dqt[1, :, rows]], axis=0).T * 0.125
+        g_send[0, j] = query.astype(BF)
+        if j in (3, 7):
+            for t, copy in back:
+                pl.when((t // 4) == (j // 4))(copy.start)
+    kept_g = k.local(g_send.at[:, k.me], g_merged.at[:, :, heads_of(k.me)])
+
+    def w_load(s):
+        cols = pl.ds(s * D, D)
+        return k.local(wq_in.at[:, :, :, :, :, cols], w_slot.at[s % 2])
+
+    w_loads = [w_load(0), w_load(1)]
+    for u in rest:
+        u.sum1()
+        u.stage2()
+    kept_g.wait()
+    for _, copy in back:
+        copy.wait_recv()
+
+    for s in range(3):
+
+        @pl.loop(0, 4)
+        def _(n):
+            cols = pl.ds(pl.multiple_of(n * 256, 256), 256)
+            block = dot(normed_t[...], g_merged[s, :, cols]).astype(BF)
+            there = pl.ds(pl.multiple_of(s * D + n * 256, 256), 256)
+            g_qkv[:, :, :, :, :, there] = block.reshape(4, 2, 2, 2, 32, 256)
+
+        last[s].stage0()
+    for u in rest:
+        u.sum2()
+        u.stage3()
+
+    for s in range(3):
+        w_loads[s].wait()
+        for n in range(4):
+            weight = w_slot[s % 2, n].reshape(256, D)
+            part = dot_nt(g_merged[s], weight)
+            cols = slice(256 * n, 256 * (n + 1))
+            if s == 0:
+                gn[:, cols] = part
+            else:
+                gn[:, cols] += part
+        if s == 0:
+            w_loads.append(w_load(2))
+    for s, u in enumerate(last):
+        cols = pl.ds(s * D, D)
+        u.add0(lambda x, yh, yl, cols=cols: g_qkv[x, yh, k.core, yl, :, cols])
+        u.stage1()
+
+    values = tokens[...].astype(F32)
+    center = values - jnp.mean(values, axis=1, keepdims=True)
+    scale = lax.rsqrt(jnp.mean(center * center, axis=1, keepdims=True) + 1e-05)
+    center = center * scale
+    grad_normed = gn[...]
+    by_gain = jnp.sum(grad_normed * center, axis=0, keepdims=True)
+    by_bias = jnp.sum(grad_normed, axis=0, keepdims=True)
+    inner = grad_normed * small_row(pack, 0)
+    part = inner - jnp.mean(inner, axis=1, keepdims=True)
+    part = part - center * jnp.mean(inner * center, axis=1, keepdims=True)
+    input_grad[...] = grad_middle[...] + part * scale
+    by_query = jnp.sum(g_merged[0].astype(F32), axis=0, keepdims=True)
+    by_value = jnp.sum(g_merged[2].astype(F32), axis=0, keepdims=True)
+    small[...] = small_in[...]
+    for x in range(4):
+        for yh in range(2):
+            n = 2 * x + yh
+            cols = slice(128 * n, 128 * (n + 1))
+            small[x, yh, 0:1, :] = by_gain[:, cols]
+            small[x, yh, 1:2, :] = by_bias[:, cols]
+            source = by_query if x < 2 else by_value
+            first = 256 * (n % 4)
+            small[x, yh, 6:7, :] = source[:, first : first + 128]
+            small[x, yh, 7:8, :] = source[:, first + 128 : first + 256]
+    small_sent = [k.to(small, small_core, k.peers("core")[0])]
+
+    for n, u in enumerate(rest):
+        u.sum3(f_rest, n)
+    gathered = [k.to(f_rest.at[k.me], f_rest.at[k.me], who) for _, who in k.rows_peers()]
+
+    small_sent[0].wait()
+    small[...] = small[...] + small_core[...]
+    coming = [
+        k.to(small.at[(k.x + j + 1) % 4], small_x.at[j], who)
+        for j, who in enumerate(k.peers("x"))
+    ]
+    small_sent += coming
+    for u in last:
+        u.sum1()
+        u.stage2()
+    wait_recv(coming)
+    small[k.x] = small[k.x] + small_x[0] + small_x[1] + small_x[2]
+    coming = [
+        k.to(small.at[k.x, ((k.y + j + 1) % 4) // 2], small_y.at[j], who)
+        for j, who in enumerate(k.peers("y"))
+    ]
+    small_sent += coming
+    for u in last:
+        u.sum2()
+        u.stage3()
+    wait_recv(coming)
+    small_z[3] = small[k.x, k.yh] + small_y[0] + small_y[1] + small_y[2]
+    coming = [k.to(small_z.at[3], small_z.at[j], who) for j, who in enumerate(k.peers("z"))]
+    small_sent += coming
+    for n, u in enumerate(last):
+        u.sum3(f_qkv, n)
+    gathered_qkv = [k.to(f_qkv.at[k.me], f_qkv.at[k.me], who) for _, who in k.rows_peers()]
+    outs = (o_qkv, o_out, o_fc1, o_fc2)
+    wait_recv(gathered)
+    for n, u in enumerate(rest):
+        u.write(f_rest, n, outs)
+    wait_recv(coming)
+    o_small[...] = small_z[0] + small_z[1] + small_z[2] + small_z[3]
+    wait_recv(gathered_qkv)
+    for n, u in enumerate(last):
+        u.write(f_qkv, n, outs)
+    for u in units:
+        u.drain()
+    wait_send(moved + [copy for _, copy in back] + small_sent[1:] + gathered + gathered_qkv)
+
+
+def backward_call(
+    g_out, g_fc1, g_fc2, grad_mixed, qkv, kx, qx, ot, lse, normed, wq, pack, tokens, grad_middle, small
+):
+    hbm = pl.BlockSpec(memory_space=pl.ANY)
+    vmem = pl.BlockSpec(memory_space=pltpu.VMEM)
+    out = jax.ShapeDtypeStruct
+    mem = pltpu.VMEM
+    return pl.pallas_call(
+        backward_kernel,
+        name="backward",
+        out_shape=(
+            out((2, 32, 3 * D), F32),
+            out((2, 32, D), F32),
+            out((2, 32, 4 * D), F32),
+            out((4, 2, 32, D), F32),
+            out((16, 128), F32),
+            out((BLK, D), F32),
+        ),
+        in_specs=[hbm, hbm, hbm, hbm, vmem, vmem, vmem, vmem, vmem, vmem, hbm, vmem, vmem, vmem, vmem],
+        out_specs=(vmem,) * 6,
+        scratch_shapes=[
+            mem((12, 4, 2, 2, 32, D), BF),
+            *[mem((count_of(order),) + R1[order], BF) for order in range(3)],
+            *[mem((count_of(order),) + R2[order], BF) for order in range(3)],
+            mem((12, 3, 32, 256), BF),
+            mem((2, 4, 2, 2, 32, D), BF),
+            mem(full_shape(3 * D), BF),
+            mem((2,) + full_shape(D), BF),
+            mem((2, LENGTH, 128), BF),
+            mem((2, 64, LENGTH), BF),
+            mem((LENGTH, 128), BF),
+            mem((2, 8, LENGTH), F32),
+            mem((2, 64, LENGTH), F32),
+            mem((3, 8, BLK, 128), BF),
+            mem((3, BLK, D), BF),
+            mem((D, BLK), BF),
+            mem((8, 32, 9 * 256), BF),
+            mem((8, 32, 3 * 256), BF),
+            mem((4, 2, 16, 128), F32),
+            mem((4, 2, 16, 128), F32),
+            mem((3, 2, 16, 128), F32),
+            mem((3, 16, 128), F32),
+            mem((4, 16, 128), F32),
+            mem((BLK, D), F32),
+            pltpu.SemaphoreType.DMA((190,)),
+            pltpu.SemaphoreType.DMA((190,)),
+        ],
+        compiler_params=pltpu.CompilerParams(
+            collective_id=1, has_side_effects=True, vmem_limit_bytes=63 * MIB
+        ),
+    )(
+        g_out.reshape(full_shape(D)),
+        g_fc1.reshape(full_shape(4 * D)),
+        g_fc2.reshape(4, 2, 2, 4, 2, 32, D),
+        grad_mixed,
+        qkv,
+        kx,
+        qx,
+        ot,
+        lse,
+        normed,
+        wq,
+        pack,
+        tokens,
+        grad_middle,
+        small,
+    )
+
+
 def layer_norm(values, gain_vec, bias_vec):
     center = values - jnp.mean(values, axis=-1, keepdims=True)
     spread = jnp.mean(center * center, axis=-1, keepdims=True)
@@ -486,30 +976,6 @@
 
 def matmul(left, right):
     return jnp.dot(left, right, preferred_element_type=jnp.float32)
-
-
-def head_slopes():
-    return 2.0 ** (-8.0 * jnp.arange(1, HEADS + 1, dtype=jnp.float32) / HEADS) * (4.0 / LENGTH)
-
-
-def key_spans(key_count):
-    width_now = 512
-    return [(offset, width_now) for offset in range(0, key_count, width_now)]
-
-
-def block_scores(query, query_seg, query_pos, key_rows, key_seg, first_key):
-    row_count = key_rows.shape[0]
-    key_count = key_rows.shape[1]
-    key_part = key_rows[:, :, :D].reshape(row_count, key_count, HEADS, HEAD_DIM)
-    value_part = key_rows[:, :, D:].reshape(row_count, key_count, HEADS, HEAD_DIM)
-    scores = jnp.einsum(
-        "rihd,rjhd->rhij", query, key_part, preferred_element_type=jnp.float32
-    ) * HEAD_DIM ** (-0.5)
-    key_pos = first_key + jnp.arange(key_count, dtype=jnp.int32)
-    distance = query_pos[:, None] - key_pos[None, :]
-    scores = scores - head_slopes()[:, None, None] * distance.astype(jnp.float32)
-    allowed = (query_seg[:, :, None] == key_seg[:, None, :]) & (distance >= 0)[None]
-    return (scores, allowed[:, None], key_part, value_part)
 
 
 def local(
@@ -529,14 +995,13 @@
     fc2_weight,
     fc2_bias,
 ):
-    row_count, block_len, _ = tokens.shape
-    flat_rows = row_count * block_len
-    full_length = block_len * lax.axis_size("ctx")
+    block_len = tokens.shape[1]
     small = small_pack(
         ln1_gain, ln1_bias, ln2_gain, ln2_bias, out_bias, fc2_bias, qkv_bias, fc1_bias
     )
-    (qkv_mat, out_mat, up_mat, down_mat, pack, normed, qkv_heads, mixed_heads, lse_heads, mixed, lse_all) = forward_call(
-        tokens.reshape(flat_rows, D),
+    flat = tokens.reshape(block_len, D)
+    (wq, wo, w1, w2, pack, normed, qkv, kx, qx, ot, lse, mixed, lse_all) = forward_call(
+        flat,
         jnp.broadcast_to(segment_ids, (8, block_len)),
         small,
         qkv_weight,
@@ -544,176 +1009,82 @@
         fc1_weight,
         fc2_weight,
     )
-    qkv_mat = qkv_mat.reshape(D, 3 * D)
-    out_mat = out_mat.reshape(D, D)
-    up_mat = up_mat.reshape(D, 4 * D)
-    down_mat = down_mat.reshape(4 * D, D)
-    gain_one_f = unpack_row(pack, 0).astype(jnp.float32)
-    bias_one_f = unpack_row(pack, 1).astype(jnp.float32)
-    gain_two_f = unpack_row(pack, 2).astype(jnp.float32)
-    bias_two_f = unpack_row(pack, 3).astype(jnp.float32)
-    out_vec = unpack_row(pack, 4)
-    down_vec = unpack_row(pack, 5)
-    qkv_vec = pack[:, :, :, 6].reshape(2 * D)
-    up_vec = pack[:, :, :, 7:9].reshape(4 * D)
-    inputs = tokens.astype(jnp.float32).reshape(flat_rows, D)
-    merged_bias = jnp.concatenate([qkv_vec[:D], jnp.zeros((D,), BF), qkv_vec[D:]]).astype(jnp.float32)
-    merged = (matmul(normed, qkv_mat) + merged_bias).astype(jnp.bfloat16)
-    query = merged[:, :D].reshape(row_count, block_len, HEADS, HEAD_DIM)
-    key_values = merged[:, D:].reshape(row_count, block_len, 2 * D)
-    query_pos = lax.axis_index("ctx") * block_len + jnp.arange(block_len, dtype=jnp.int32)
+    out_mat = wo.reshape(D, D)
+    up_mat = w1.reshape(D, 4 * D)
+    down_mat = w2.reshape(4 * D, D)
+    gain_two = unpack_row(pack, 2).astype(jnp.float32)
+    bias_two = unpack_row(pack, 3).astype(jnp.float32)
+    out_vec = unpack_row(pack, 4).astype(jnp.float32)
+    down_vec = unpack_row(pack, 5).astype(jnp.float32)
+    up_vec = pack[:, :, :, 7:9].reshape(4 * D).astype(jnp.float32)
     log_sums = lse_all[:, :, 0].reshape(1, HEADS, block_len)
-    mixed_exact = mixed.astype(jnp.float32).reshape(row_count, block_len, HEADS, HEAD_DIM)
-    middle = inputs + matmul(mixed, out_mat) + out_vec.astype(jnp.float32)
-    normed_two = layer_norm(middle, gain_two_f, bias_two_f).astype(jnp.bfloat16)
-    hidden = matmul(normed_two, up_mat) + up_vec.astype(jnp.float32)
+
+    middle = flat.astype(jnp.float32) + matmul(mixed, out_mat) + out_vec
+    normed_two = layer_norm(middle, gain_two, bias_two).astype(jnp.bfloat16)
+    hidden = matmul(normed_two, up_mat) + up_vec
     active = gelu_tanh(hidden).astype(jnp.bfloat16)
-    output = middle + matmul(active, down_mat) + down_vec.astype(jnp.float32)
-    qkv_back, out_back, up_back, down_back = qkv_mat, out_mat, up_mat, down_mat
-    grad_down = cotangent.reshape(flat_rows, D)
+    output = middle + matmul(active, down_mat) + down_vec
+
+    grad_down = cotangent.reshape(block_len, D)
     grad_output = grad_down.astype(jnp.float32)
-    fc2_weight_grad = matmul_tn(active, grad_down)
+    g_fc2 = matmul_tn(active, grad_down).astype(jnp.bfloat16)
     fc2_bias_grad = jnp.sum(grad_output, axis=0)
-    grad_active = matmul_nt(grad_down, down_back)
+    grad_active = matmul_nt(grad_down, down_mat)
     _, gelu_pull = jax.vjp(gelu_tanh, hidden)
     grad_hidden = gelu_pull(grad_active)[0].astype(jnp.bfloat16)
-    fc1_weight_grad = matmul_tn(normed_two, grad_hidden)
+    g_fc1 = matmul_tn(normed_two, grad_hidden).astype(jnp.bfloat16)
     fc1_bias_grad = jnp.sum(grad_hidden.astype(jnp.float32), axis=0)
-    grad_normed_two = matmul_nt(grad_hidden, up_back)
-    _, norm_pull_two = jax.vjp(layer_norm, middle, gain_two_f, bias_two_f)
-    grad_middle_part, ln2_gain_grad, ln2_bias_grad = norm_pull_two(grad_normed_two)
-    grad_middle = grad_output + grad_middle_part
+    grad_normed_two = matmul_nt(grad_hidden, up_mat)
+    _, norm_pull = jax.vjp(layer_norm, middle, gain_two, bias_two)
+    part, ln2_gain_grad, ln2_bias_grad = norm_pull(grad_normed_two)
+    grad_middle = grad_output + part
     grad_branch = grad_middle.astype(jnp.bfloat16)
-    out_weight_grad = matmul_tn(mixed, grad_branch)
+    g_out = matmul_tn(mixed, grad_branch).astype(jnp.bfloat16)
     out_bias_grad = jnp.sum(grad_branch.astype(jnp.float32), axis=0)
-    grad_mixed = (
-        matmul_nt(grad_branch, out_back)
-        .astype(jnp.bfloat16)
-        .reshape(row_count, block_len, HEADS, HEAD_DIM)
-    )
-    delta = jnp.swapaxes(jnp.sum(grad_mixed.astype(jnp.float32) * mixed_exact, axis=-1), 1, 2)
-    first_row = jnp.int32(0)
-    grad_query = jnp.zeros((row_count, block_len, HEADS, HEAD_DIM), jnp.float32)
-    grad_keys = jnp.zeros((row_count, full_length, 2 * D), jnp.float32)
-    key_rows = lax.all_gather(key_values, "ctx", axis=1, tiled=True)
-    key_seg = lax.all_gather(segment_ids, "ctx", axis=1, tiled=True)
-    for offset, width_now in key_spans(key_rows.shape[1]):
-        scores, allowed, key_part, value_part = block_scores(
-            query,
-            segment_ids,
-            query_pos,
-            key_rows[:, offset : offset + width_now],
-            key_seg[:, offset : offset + width_now],
-            first_row + offset,
-        )
-        probs = jnp.where(allowed, jnp.exp(scores - log_sums[..., None]), 0.0)
-        grad_probs = jnp.einsum(
-            "rihd,rjhd->rhij", grad_mixed, value_part, preferred_element_type=jnp.float32
-        )
-        grad_scores = (probs * (grad_probs - delta[..., None])).astype(jnp.bfloat16)
-        grad_query = grad_query + jnp.einsum(
-            "rhij,rjhd->rihd", grad_scores, key_part, preferred_element_type=jnp.float32
-        ) * HEAD_DIM ** (-0.5)
-        grad_key = jnp.einsum(
-            "rhij,rihd->rjhd", grad_scores, query, preferred_element_type=jnp.float32
-        ) * HEAD_DIM ** (-0.5)
-        grad_value = jnp.einsum(
-            "rhij,rihd->rjhd",
-            probs.astype(jnp.bfloat16),
-            grad_mixed,
-            preferred_element_type=jnp.float32,
-        )
-        key_term = jnp.concatenate(
-            [
-                grad_key.reshape(row_count, width_now, D),
-                grad_value.reshape(row_count, width_now, D),
-            ],
-            axis=-1,
-        )
-        place_at = first_row + offset
-        previous = lax.dynamic_slice_in_dim(grad_keys, place_at, width_now, 1)
-        grad_keys = lax.dynamic_update_slice_in_dim(grad_keys, previous + key_term, place_at, 1)
-    grad_query, grad_keys = (grad_query, grad_keys)
-    own_key_grads = lax.psum_scatter(
-        grad_keys.astype(jnp.bfloat16), "ctx", scatter_dimension=1, tiled=True
-    ).astype(jnp.float32)
-    grad_merged = jnp.concatenate(
-        [grad_query.reshape(flat_rows, D), own_key_grads.reshape(flat_rows, 2 * D)], axis=-1
-    ).astype(jnp.bfloat16)
-    qkv_weight_grad = matmul_tn(normed, grad_merged)
-    merged_sums = jnp.sum(grad_merged.astype(jnp.float32), axis=0)
-    qkv_bias_grad = jnp.concatenate([merged_sums[:D], merged_sums[2 * D :]])
-    grad_normed = matmul_nt(grad_merged, qkv_back)
-    _, norm_pull_one = jax.vjp(layer_norm, inputs, gain_one_f, bias_one_f)
-    grad_input_part, ln1_gain_grad, ln1_bias_grad = norm_pull_one(grad_normed)
-    input_grad = (grad_middle + grad_input_part).reshape(row_count, block_len, D)
-    shard_grads = (
-        lax.psum_scatter(
-            ln1_gain_grad.astype(jnp.bfloat16), "fsdp", scatter_dimension=0, tiled=True
-        ).astype(jnp.float32),
-        lax.psum_scatter(
-            ln1_bias_grad.astype(jnp.bfloat16), "fsdp", scatter_dimension=0, tiled=True
-        ).astype(jnp.float32),
-        lax.psum_scatter(
-            qkv_weight_grad.astype(jnp.bfloat16), "fsdp", scatter_dimension=0, tiled=True
-        ).astype(jnp.float32),
-        lax.psum_scatter(
-            qkv_bias_grad.astype(jnp.bfloat16), "fsdp", scatter_dimension=0, tiled=True
-        ).astype(jnp.float32),
-        lax.psum_scatter(
-            out_weight_grad.astype(jnp.bfloat16), "fsdp", scatter_dimension=0, tiled=True
-        ).astype(jnp.float32),
-        lax.psum_scatter(
-            out_bias_grad.astype(jnp.bfloat16), "fsdp", scatter_dimension=0, tiled=True
-        ).astype(jnp.float32),
-        lax.psum_scatter(
-            ln2_gain_grad.astype(jnp.bfloat16), "fsdp", scatter_dimension=0, tiled=True
-        ).astype(jnp.float32),
-        lax.psum_scatter(
-            ln2_bias_grad.astype(jnp.bfloat16), "fsdp", scatter_dimension=0, tiled=True
-        ).astype(jnp.float32),
-        lax.psum_scatter(
-            fc1_weight_grad.astype(jnp.bfloat16), "fsdp", scatter_dimension=0, tiled=True
-        ).astype(jnp.float32),
-        lax.psum_scatter(
-            fc1_bias_grad.astype(jnp.bfloat16), "fsdp", scatter_dimension=0, tiled=True
-        ).astype(jnp.float32),
-        lax.psum_scatter(
-            fc2_weight_grad.astype(jnp.bfloat16), "fsdp", scatter_dimension=0, tiled=True
-        ).astype(jnp.float32),
-        lax.psum_scatter(
-            fc2_bias_grad.astype(jnp.bfloat16), "fsdp", scatter_dimension=0, tiled=True
-        ).astype(jnp.float32),
-    )
-    g_one, b_one, g_qkv, g_qkvb, g_out, g_outb, g_two, b_two, g_up, g_upb, g_down, g_downb = (
-        lax.psum(shard_grads[0].astype(jnp.bfloat16), "ctx").astype(jnp.float32),
-        lax.psum(shard_grads[1].astype(jnp.bfloat16), "ctx").astype(jnp.float32),
-        lax.psum(shard_grads[2].astype(jnp.bfloat16), "ctx").astype(jnp.float32),
-        lax.psum(shard_grads[3].astype(jnp.bfloat16), "ctx").astype(jnp.float32),
-        lax.psum(shard_grads[4].astype(jnp.bfloat16), "ctx").astype(jnp.float32),
-        lax.psum(shard_grads[5].astype(jnp.bfloat16), "ctx").astype(jnp.float32),
-        lax.psum(shard_grads[6].astype(jnp.bfloat16), "ctx").astype(jnp.float32),
-        lax.psum(shard_grads[7].astype(jnp.bfloat16), "ctx").astype(jnp.float32),
-        lax.psum(shard_grads[8].astype(jnp.bfloat16), "ctx").astype(jnp.float32),
-        lax.psum(shard_grads[9].astype(jnp.bfloat16), "ctx").astype(jnp.float32),
-        lax.psum(shard_grads[10].astype(jnp.bfloat16), "ctx").astype(jnp.float32),
-        lax.psum(shard_grads[11].astype(jnp.bfloat16), "ctx").astype(jnp.float32),
-    )
+    grad_mixed = matmul_nt(grad_branch, out_mat).astype(jnp.bfloat16)
+
+    four = jnp.stack([ln2_gain_grad, ln2_bias_grad, out_bias_grad, fc2_bias_grad])
+    four = four.reshape(4, 4, 2, 128).transpose(1, 2, 0, 3)
+    none = jnp.zeros((4, 2, 2, 128), jnp.float32)
+    small_grads = jnp.concatenate(
+        [none, four, none, fc1_bias_grad.reshape(4, 2, 4, 128), none, none], axis=2
+    )
+    g_qkv, g_wo, g_up, g_down, small_sums, input_grad = backward_call(
+        g_out,
+        g_fc1,
+        g_fc2,
+        grad_mixed,
+        qkv,
+        kx,
+        qx,
+        ot,
+        lse,
+        normed,
+        wq,
+        pack,
+        flat,
+        grad_middle,
+        small_grads,
+    )
+    core = lax.axis_index("fsdp") % 2
+    halves = lax.dynamic_slice_in_dim(small_sums[:6], core * 64, 64, 1)
+    g_qkvb = lax.dynamic_slice_in_dim(small_sums, 6 + core, 1, 0).reshape(128)
+    g_upb = lax.dynamic_slice_in_dim(small_sums, 8 + 2 * core, 2, 0).reshape(256)
     return (
-        output.astype(jnp.bfloat16).reshape(row_count, block_len, D),
-        input_grad,
-        g_one,
-        b_one,
-        g_qkv,
+        output.astype(jnp.bfloat16).reshape(1, block_len, D),
+        input_grad.reshape(1, block_len, D),
+        halves[0],
+        halves[1],
+        g_qkv.reshape(64, 3 * D),
         g_qkvb,
-        g_out,
-        g_outb,
-        g_two,
-        b_two,
-        g_up,
+        g_wo.reshape(64, D),
+        halves[4],
+        halves[2],
+        halves[3],
+        g_up.reshape(64, 4 * D),
         g_upb,
-        g_down,
-        g_downb,
+        g_down.reshape(256, D),
+        halves[5],
         log_sums,
     )
 

time: 941 us -> 331 us (0.35)
  waiting for transfers between devices: 456 us -> 0 us
  Pallas kernels: 135 us -> 262 us
  blocking collectives: 101 us -> 0 us
  matrix products: 113 us -> 38.5 us
  other arithmetic: 56.2 us -> 1.79 us
  local copies, waits for them, and re-layouts: 52.6 us -> 21.4 us
  between operations: 17.3 us -> 1.24 us
    reduce_scatter x5 -> x0, waiting for transfers between devices: 419 us -> none  [the longest x1 106 us: local(): lax.psum_scatter(fc2_weight_grad.astype(jnp.bfloat16), 'fsdp', scatter_di...]
    pallas_call x0 -> x1, Pallas kernels: none -> 127 us  [backward_call(): pl.pallas_call(backward_kernel, name='backward', out_shape=(out((2, 32, 3...]
    unnamed x1 -> x0, blocking collectives: 66 us -> none
    dot_general x20 -> x0, matrix products: 50.4 us -> none  [the longest x4 16.1 us: local(): jnp.einsum('rihd,rjhd->rhij', grad_mixed, value_part, preferred_element_t...]
    all_gather x1 -> x0, waiting for transfers between devices: 37.4 us -> none  [local(): key_rows = lax.all_gather(key_values, 'ctx', axis=1, tiled=True)]
    slice x16 -> x2, local copies, waits for them, and re-layouts: 26.7 us -> 0.69 us  [the longest x1 0.67 us: local(): halves = lax.dynamic_slice_in_dim(small_sums[:6], core * 64, 64, 1)]
    convert_element_type x17 -> x2, other arithmetic: 23.2 us -> 0.04 us  [the longest x1 0.03 us: local(): gain_two = unpack_row(pack, 2).astype(jnp.float32)]
    psum x1 -> x0, blocking collectives: 19.5 us -> none  [local(): lax.psum(shard_grads[0].astype(jnp.bfloat16), 'ctx').astype(jnp.float32)]
  transfers between devices with their start and end apart: 7 -> 0, of which waited for: 6 -> 0; matrix products, arithmetic and copies ran while one was open for 10% -> 0% of each run, Pallas kernels for 0% -> 0%
where the time goes in v2:
time: 331 us; the launch traced here: 325 us
  Pallas kernels  262 us (79%)
  matrix products  38.5 us (12%)
  local copies, waits for them, and re-layouts  21.4 us (6%)
    pallas_call x1, Pallas kernels, forward_call(): pl.pallas_call(forward_kernel, name='forward', out_shape=(out(full_shape(...  135 us
    pallas_call x1, Pallas kernels, backward_call(): pl.pallas_call(backward_kernel, name='backward', out_shape=(out((2, 32, 3...  127 us
    dot_general x3, matrix products, matmul_tn(): lax.dot_general(left, right, (((0,), (0,)), ((), ())), preferred_element_...  16.5 us
    unnamed x50, local copies, waits for them, and re-layouts  14.7 us
    dot_general x3, matrix products, matmul(): return jnp.dot(left, right, preferred_element_type=jnp.float32)  12.4 us
    dot_general x3, matrix products, matmul_nt(): lax.dot_general(left, right, (((1,), (1,)), ((), ())), preferred_element_...  9.65 us

profile of v2, /device:TPU:0, one launch (start us, length us, event | category | flops | bytes accessed | tf_op | source)
XLA Modules:
  0.0 325.0 jit_solution(1530044911920223956)
XLA Ops:
  0.8 0.8 stack.42
  1.6 0.7 maximum_maximum_fusion.small
  2.3 0.7 broadcast_in_dim.15.seg
  3.0 1.0 copy-done
  4.1 1.0 copy-done.2
  5.1 1.0 copy-done.3
  6.1 1.0 copy-done.4
  7.1 0.9 copy-done.7
  8.0 135.5 %forward.1 = (bf16[4,2,2,2,32,3072]{5,4,3,2,1,0:T(8,128)(2,1)}, bf16[4,2,2,2,32,1024]{5,4,3,2,1,0:T(8,128)(2,1)}, bf16[4,2,2,2,32,4096]{5,4,3,2,1,0:T(8,128)(2,1...) custom-call(bf16[256,1024]{1,0:T(8,128)(2,1)S(1)} %bitcast.83, ...), custom_call_target="tpu_custom_call" | custom-call | tf_op jit(solution)/shard_map/forward/pallas_call | solution.py:404
  143.6 0.7 copy.30
  144.4 2.4 fusion.18
  147.1 6.3 %convolution_add_fusion = f32[256,4096]{1,0:T(8,128)S(1)} fusion(bf16[1024,4096]{1,0:T(8,128)(2,1)} %bitcast.122, f32[4096]{0:T(1024)S(1)} %convert.5, f32[256,1024]{1,0:T(8,128)S(1)} %get-tuple-element.87, f32[1024]{0:T(1024)S(1)} %bitcast.102, f32[1024]{0:T(1024)S(1)} %bitcast.98, f32[256]{0:T(256)S(1)} %fusion.13, f32[256]{0:T(256)S(1)} %broadcast_multiply_fusion), kind=kOutput, calls=%fused_computation.5 | convolution fusion | flops 2149842944 | bytes 13658112 | tf_op jit(solution)/shard_map/dot_general | solution.py:978
  153.6 3.6 %fusion.10 = bf16[1,256,1024]{2,1,0:T(8,128)(2,1)} fusion(f32[256,1024]{1,0:T(8,128)S(1)} %get-tuple-element.87, bf16[4096,1024]{1,0:T(8,128)(2,1)S(1)} %bitcast.128, f32[1024]{0:T(1024)S(1)} %bitcast.109, f32[256,4096]{1,0:T(8,128)S(1)} %convolution_add_fusion), kind=kOutput, calls=%fused_computation.25 | convolution fusion | flops 2157707264 | bytes 14159872 | tf_op jit(solution)/shard_map/dot_general | solution.py:978
  157.2 5.4 %convert_reduce_fusion = (f32[4096]{0:T(1024)S(1)}, bf16[256,4096]{1,0:T(8,128)(2,1)S(1)}) fusion(f32[256,4096]{1,0:T(8,128)S(1)} %convolution_add_fusion, bf16[4096,1024]{1,0:T(8,128)(2,1)S(1)} %bitcast.129, bf16[1,256,1024]{2,1,0:T(8,128)(2,1)S(1)} %copy-done.16), kind=kOutput, calls=%fused_computation.13 | convolution fusion | flops 2170548224 | bytes 15220736 | tf_op jit(solution)/shard_map/dot_general | solution.py:972
  162.7 2.7 multiply_reduce_fusion
  165.4 0.4 fusion.17
  166.1 0.9 copy-done.13
  167.0 1.5 convolution_convert_fusion.3.grad_mixed
  168.6 1.3 concatenate.20.small_in
  169.8 2.1 convolution_convert_fusion.2
  171.9 8.6 %convolution_convert_fusion = bf16[4096,1024]{1,0:T(8,128)(2,1)} fusion(bf16[1,256,1024]{2,1,0:T(8,128)(2,1)S(1)} %copy-done.16, f32[256,4096]{1,0:T(8,128)} %copy-done.17), kind=kOutput, calls=%fused_computation | convolution fusion | flops 2161115136 | bytes 13107200 | tf_op jit(solution)/shard_map/dot_general | solution.py:966
  180.6 5.8 %convolution_convert_fusion.1 = bf16[1024,4096]{1,0:T(8,128)(2,1)} fusion(bf16[256,4096]{1,0:T(8,128)(2,1)S(1)} %copy-done.12, f32[256,1024]{1,0:T(8,128)S(1)} %copy-done.10, f32[1024]{0:T(1024)S(1)} %bitcast.103, f32[1024]{0:T(1024)S(1)} %bitcast.101, f32[256]{0:T(256)S(1)} %fusion.13, f32[256]{0:T(256)S(1)} %broadcast_multiply_fusion), kind=kOutput, calls=%fused_computation.1 | convolution fusion | flops 2152988672 | bytes 11544576 | tf_op jit(solution)/shard_map/dot_general | solution.py:966
  186.3 126.5 %backward.1 = (f32[2,32,3072]{2,1,0:T(8,128)}, f32[2,32,1024]{2,1,0:T(8,128)}, f32[2,32,4096]{2,1,0:T(8,128)}, f32[4,2,32,1024]{3,2,1,0:T(8,128)}, f32[16,128]{1,0:T(8,128)}, /*index=5*/f32[256,1024]{1,0:T(8,128)}) custom-call(bf16[4,2,2,2,32,1024]{5,4,3,2,1,0:T(8,128)(2,1)} %bitcast.89, bf16[4,2,2,2,32,4096]{5,4,3,2,1,0:T(8,128)(2,1)} %bitcast.88, ...), custom_call_target="tpu_custom_call" | custom-call | tf_op jit(solution)/shard_map/backward/pallas_call | solution.py:893
  312.9 1.3 fusion.14
  314.2 1.2 dynamic-slice_bitcast_fusion
  315.5 0.7 slice.60
  316.2 0.5 slice_bitcast_fusion
  316.8 2.3 copy.36
  319.1 2.1 copy.37
  321.1 1.7 copy.38
  322.8 1.0 copy.39
  323.8 1.0 copy.40
  (57 shorter events, 0.9 us)
Async XLA Ops:
  3.0 1.0 copy-start
  4.1 1.0 copy-start.2
  5.1 1.0 copy-start.3
  6.1 1.0 copy-start.4
  7.1 0.9 copy-start.7
  143.5 9.9 %copy-start.1 = (bf16[256,1024]{1,0:T(8,128)(2,1)}, bf16[256,1024]{1,0:T(8,128)(2,1)S(1)}, u32[]{:S(2)}) copy-start(bf16[256,1024]{1,0:T(8,128)(2,1)S(1)} %get-tuple-element.44.normed) | copy-start | bytes 1572868
  143.6 9.9 %copy-start.5 = (bf16[4,2,2,16,128]{4,3,2,1,0:T(8,128)(2,1)}, bf16[4,2,2,16,128]{4,3,2,1,0:T(8,128)(2,1)S(1)}, u32[]{:S(2)}) copy-start(bf16[4,2,2,16,128]{4,3,2,1,0:T(8,128)(2,1)S(1)} %get-tuple-element.36.pack) | copy-start | bytes 196612
  143.6 9.9 %copy-start.6 = (f32[2,8,2048]{2,1,0:T(8,128)}, f32[2,8,2048]{2,1,0:T(8,128)S(1)}, u32[]{:S(2)}) copy-start(f32[2,8,2048]{2,1,0:T(8,128)S(1)} %get-tuple-element.43.lse) | copy-start | bytes 393220
  146.8 18.6 %copy-start.9 = (f32[256,1024]{1,0:T(8,128)}, f32[256,1024]{1,0:T(8,128)S(1)}, u32[]{:S(2)}) copy-start(f32[256,1024]{1,0:T(8,128)S(1)} %get-tuple-element.87) | copy-start | bytes 3145732
  146.8 6.7 %slice-start.2 = ((s8[8388608]{0:T(1024)(128)(4,1)}), s8[4194304]{0:T(1024)(128)(4,1)S(1)}, s32[]{:S(2)}) async-start(s8[8388608]{0:T(1024)(128)(4,1)} %bitcast.126), calls=%async_computation.2 | async-start | bytes 8388608
  147.1 6.4 %slice-start.3 = ((s8[8388608]{0:T(1024)(128)(4,1)}), s8[4194304]{0:T(1024)(128)(4,1)S(1)}, s32[]{:S(2)}) async-start(s8[8388608]{0:T(1024)(128)(4,1)} %bitcast.126), calls=%async_computation.3 | async-start | bytes 8388608
  153.5 3.7 %copy-start.17 = (f32[256,4096]{1,0:T(8,128)}, f32[256,4096]{1,0:T(8,128)S(1)}, u32[]{:S(2)}) copy-start(f32[256,4096]{1,0:T(8,128)S(1)} %convolution_add_fusion) | copy-start | bytes 12582916
  153.5 3.7 %copy-start.16 = (bf16[1,256,1024]{2,1,0:T(8,128)(2,1)S(1)}, bf16[1,256,1024]{2,1,0:T(8,128)(2,1)}, u32[]{:S(2)}) copy-start(bf16[1,256,1024]{2,1,0:T(8,128)(2,1)} %param.17) | copy-start | bytes 1572868
  153.5 9.1 %slice-start = ((s8[8388608]{0:T(1024)(128)(4,1)}), s8[4194304]{0:T(1024)(128)(4,1)S(1)}, s32[]{:S(2)}) async-start(s8[8388608]{0:T(1024)(128)(4,1)} %bitcast.123), calls=%async_computation | async-start | bytes 8388608
  157.2 5.5 %slice-start.1 = ((s8[8388608]{0:T(1024)(128)(4,1)}), s8[4194304]{0:T(1024)(128)(4,1)S(1)}, s32[]{:S(2)}) async-start(s8[8388608]{0:T(1024)(128)(4,1)} %bitcast.123), calls=%async_computation.1 | async-start | bytes 8388608
  162.6 2.7 copy-start.11
  165.4 1.6 copy-start.13
  166.1 14.5 %copy-start.8 = (f32[256,1024]{1,0:T(8,128)}, f32[256,1024]{1,0:T(8,128)S(1)}, u32[]{:S(2)}) copy-start(f32[256,1024]{1,0:T(8,128)S(1)} %get-tuple-element.72.grad_middle) | copy-start | bytes 3145732
  171.9 8.6 %copy-start.10 = (f32[256,1024]{1,0:T(8,128)S(1)}, f32[256,1024]{1,0:T(8,128)}, u32[]{:S(2)}) copy-start(f32[256,1024]{1,0:T(8,128)} %copy-done.9) | copy-start | bytes 3145732
  171.9 8.6 %copy-start.12 = (bf16[256,4096]{1,0:T(8,128)(2,1)S(1)}, bf16[256,4096]{1,0:T(8,128)(2,1)}, u32[]{:S(2)}) copy-start(bf16[256,4096]{1,0:T(8,128)(2,1)} %copy-done.11) | copy-start | bytes 6291460
  312.9 9.9 %copy-start.15 = (f32[2,32,4096]{2,1,0:T(8,128)S(1)}, f32[2,32,4096]{2,1,0:T(8,128)}, u32[]{:S(2)}) copy-start(f32[2,32,4096]{2,1,0:T(8,128)} %get-tuple-element.50) | copy-start | bytes 3145732
  312.9 10.9 %copy-start.14 = (f32[4,2,32,1024]{3,2,1,0:T(8,128)S(1)}, f32[4,2,32,1024]{3,2,1,0:T(8,128)}, u32[]{:S(2)}) copy-start(f32[4,2,32,1024]{3,2,1,0:T(8,128)} %get-tuple-element.51) | copy-start | bytes 3145732

commit v3 on v2

--- a/solution.py
+++ b/solution.py
@@ -313,6 +313,8 @@
     part = pack.at[:, :, k.core]
     small_c = [k.to(part, part, k.peers("core")[0])]
 
+    for g in rest:
+        g.stage2()
     values = tokens[...].astype(F32)
     center = values - jnp.mean(values, axis=1, keepdims=True)
     center = center * lax.rsqrt(jnp.mean(center * center, axis=1, keepdims=True) + 1e-05)
@@ -327,8 +329,6 @@
     )
     for g in first:
         g.cross()
-    for g in rest:
-        g.stage2()
     for g in first:
         g.finish()
     kept.append(k.local(wq, wq_out))
@@ -367,6 +367,10 @@
         @pl.loop(0, 2)
         def _(h):
             attend(k, kx, qx, vt, ot, lse, h, i)
+        if i == 5:
+            for g in rest:
+                if g.order == 0:
+                    g.cross()
 
         both = jnp.concatenate(
             [ot[0, :, BLK * i : BLK * (i + 1)], ot[1, :, BLK * i : BLK * (i + 1)]], axis=0
@@ -382,7 +386,8 @@
         part = pl.ds(pl.multiple_of(t * BLK, BLK), BLK)
         back.append(k.to(lse.at[:, :, part], lse_all.at[k.me], who))
     for g in rest:
-        g.cross()
+        if g.order != 0:
+            g.cross()
     wait_recv(back)
     for g in rest:
         g.finish()
@@ -434,7 +439,7 @@
             pltpu.SemaphoreType.DMA((170,)),
         ],
         compiler_params=pltpu.CompilerParams(
-            collective_id=0, has_side_effects=True, vmem_limit_bytes=50 * MIB
+            collective_id=0, has_side_effects=True, vmem_limit_bytes=62 * MIB
         ),
     )(
         tokens,

time: 331 us -> 319 us (0.964)
  Pallas kernels: 262 us -> 251 us
    pallas_call x1, Pallas kernels: 135 us -> 125 us  [forward_call(): pl.pallas_call(forward_kernel, name='forward', out_shape=(out(full_shape(...]
    unnamed x50 -> x32, local copies, waits for them, and re-layouts: 14.7 us -> 9.5 us
where the time goes in v3:
time: 319 us; the launch traced here: 313 us
  Pallas kernels  251 us (79%)
  matrix products  38.1 us (12%)
  local copies, waits for them, and re-layouts  18.6 us (6%)
  other arithmetic  3.35 us (1%)
    pallas_call x1, Pallas kernels, backward_call(): pl.pallas_call(backward_kernel, name='backward', out_shape=(out((2, 32, 3...  126 us
    pallas_call x1, Pallas kernels, forward_call(): pl.pallas_call(forward_kernel, name='forward', out_shape=(out(full_shape(...  125 us
    dot_general x3, matrix products, matmul_tn(): lax.dot_general(left, right, (((0,), (0,)), ((), ())), preferred_element_...  16.4 us
    dot_general x3, matrix products, matmul(): return jnp.dot(left, right, preferred_element_type=jnp.float32)  12.2 us
    unnamed x32, local copies, waits for them, and re-layouts  9.5 us
    dot_general x3, matrix products, matmul_nt(): lax.dot_general(left, right, (((1,), (1,)), ((), ())), preferred_element_...  9.49 us

profile of v3, /device:TPU:0, one launch (start us, length us, event | category | flops | bytes accessed | tf_op | source)
XLA Modules:
  0.0 312.6 jit_solution(10631942380580113208)
XLA Ops:
  0.8 0.8 stack.42
  1.6 1.3 maximum_maximum_fusion.small
  2.9 1.3 broadcast_in_dim.15.seg
  4.2 125.1 %forward.1 = (bf16[4,2,2,2,32,3072]{5,4,3,2,1,0:T(8,128)(2,1)}, bf16[4,2,2,2,32,1024]{5,4,3,2,1,0:T(8,128)(2,1)}, bf16[4,2,2,2,32,4096]{5,4,3,2,1,0:T(8,128)(2,1...) custom-call(bf16[256,1024]{1,0:T(8,128)(2,1)} %bitcast.85, ...), custom_call_target="tpu_custom_call" | custom-call | tf_op jit(solution)/shard_map/forward/pallas_call | solution.py:409
  129.3 0.9 slice.57
  130.2 0.9 slice.67
  131.1 0.6 copy.30
  131.7 1.0 add_convert_fusion.3
  132.7 2.6 fusion.18
  135.3 0.2 multiply_reduce_fusion.2
  135.6 6.0 %convolution_add_fusion = f32[256,4096]{1,0:T(8,128)S(1)} fusion(bf16[1024,4096]{1,0:T(8,128)(2,1)} %bitcast.122, f32[4096]{0:T(1024)S(1)} %convert.5, f32[256,1024]{1,0:T(8,128)S(1)} %get-tuple-element.87, f32[1024]{0:T(1024)S(1)} %bitcast.102, f32[1024]{0:T(1024)S(1)} %bitcast.97, f32[256]{0:T(256)S(1)} %fusion.13, f32[256]{0:T(256)S(1)} %broadcast_multiply_fusion), kind=kOutput, calls=%fused_computation.5 | convolution fusion | flops 2149842944 | bytes 13658112 | tf_op jit(solution)/shard_map/dot_general | solution.py:983
  141.6 3.6 %fusion.10 = bf16[1,256,1024]{2,1,0:T(8,128)(2,1)} fusion(f32[256,1024]{1,0:T(8,128)S(1)} %get-tuple-element.87, bf16[4096,1024]{1,0:T(8,128)(2,1)S(1)} %bitcast.128, f32[1024]{0:T(1024)S(1)} %bitcast.109, f32[256,4096]{1,0:T(8,128)S(1)} %convolution_add_fusion), kind=kOutput, calls=%fused_computation.25 | convolution fusion | flops 2157707264 | bytes 14159872 | tf_op jit(solution)/shard_map/dot_general | solution.py:983
  145.2 5.2 %convert_reduce_fusion = (f32[4096]{0:T(1024)S(1)}, bf16[256,4096]{1,0:T(8,128)(2,1)S(1)}) fusion(f32[256,4096]{1,0:T(8,128)S(1)} %convolution_add_fusion, bf16[4096,1024]{1,0:T(8,128)(2,1)S(1)} %bitcast.129, bf16[1,256,1024]{2,1,0:T(8,128)(2,1)S(1)} %copy-done.6), kind=kOutput, calls=%fused_computation.13 | convolution fusion | flops 2170548224 | bytes 15220736 | tf_op jit(solution)/shard_map/dot_general | solution.py:977
  150.5 2.7 multiply_reduce_fusion
  153.2 0.4 fusion.17
  153.6 0.3 convert_reduce_fusion.2
  153.9 0.9 copy-done.3
  154.8 1.6 convolution_convert_fusion.3.grad_mixed
  156.4 1.3 concatenate.20.small_in
  157.7 2.1 convolution_convert_fusion.2
  159.8 8.6 %convolution_convert_fusion = bf16[4096,1024]{1,0:T(8,128)(2,1)} fusion(bf16[1,256,1024]{2,1,0:T(8,128)(2,1)S(1)} %copy-done.6, f32[256,4096]{1,0:T(8,128)} %copy-done.8), kind=kOutput, calls=%fused_computation | convolution fusion | flops 2161115136 | bytes 13107200 | tf_op jit(solution)/shard_map/dot_general | solution.py:971
  168.4 5.8 %convolution_convert_fusion.1 = bf16[1024,4096]{1,0:T(8,128)(2,1)} fusion(bf16[256,4096]{1,0:T(8,128)(2,1)S(1)} %copy-done.2, f32[256,1024]{1,0:T(8,128)S(1)} %get-tuple-element.87, f32[1024]{0:T(1024)S(1)} %bitcast.103, f32[1024]{0:T(1024)S(1)} %bitcast.100, f32[256]{0:T(256)S(1)} %fusion.13, f32[256]{0:T(256)S(1)} %broadcast_multiply_fusion), kind=kOutput, calls=%fused_computation.1 | convolution fusion | flops 2152988672 | bytes 11544576 | tf_op jit(solution)/shard_map/dot_general | solution.py:971
  174.1 126.4 %backward.1 = (f32[2,32,3072]{2,1,0:T(8,128)}, f32[2,32,1024]{2,1,0:T(8,128)}, f32[2,32,4096]{2,1,0:T(8,128)}, f32[4,2,32,1024]{3,2,1,0:T(8,128)}, f32[16,128]{1,0:T(8,128)}, /*index=5*/f32[256,1024]{1,0:T(8,128)}) custom-call(bf16[4,2,2,2,32,1024]{5,4,3,2,1,0:T(8,128)(2,1)} %bitcast.83, bf16[4,2,2,2,32,4096]{5,4,3,2,1,0:T(8,128)(2,1)} %bitcast.82, ...), custom_call_target="tpu_custom_call" | custom-call | tf_op jit(solution)/shard_map/backward/pallas_call | solution.py:898
  300.5 1.3 fusion.14
  301.9 1.2 dynamic-slice_bitcast_fusion
  303.1 0.7 slice.60
  303.9 0.5 slice_bitcast_fusion
  304.4 2.3 copy.36
  306.7 2.1 copy.37
  308.8 1.7 copy.38
  310.5 1.0 copy.39
  311.4 1.0 copy.40
  (39 shorter events, 0.4 us)
Async XLA Ops:
  135.3 6.3 %slice-start.2 = ((s8[8388608]{0:T(1024)(128)(4,1)}), s8[4194304]{0:T(1024)(128)(4,1)S(1)}, s32[]{:S(2)}) async-start(s8[8388608]{0:T(1024)(128)(4,1)} %bitcast.126), calls=%async_computation.2 | async-start | bytes 8388608
  135.6 6.0 %slice-start.3 = ((s8[8388608]{0:T(1024)(128)(4,1)}), s8[4194304]{0:T(1024)(128)(4,1)S(1)}, s32[]{:S(2)}) async-start(s8[8388608]{0:T(1024)(128)(4,1)} %bitcast.126), calls=%async_computation.3 | async-start | bytes 8388608
  141.6 3.6 %copy-start.8 = (f32[256,4096]{1,0:T(8,128)}, f32[256,4096]{1,0:T(8,128)S(1)}, u32[]{:S(2)}) copy-start(f32[256,4096]{1,0:T(8,128)S(1)} %convolution_add_fusion) | copy-start | bytes 12582916
  141.6 3.6 %copy-start.6 = (bf16[1,256,1024]{2,1,0:T(8,128)(2,1)S(1)}, bf16[1,256,1024]{2,1,0:T(8,128)(2,1)}, u32[]{:S(2)}) copy-start(bf16[1,256,1024]{2,1,0:T(8,128)(2,1)} %param.17) | copy-start | bytes 1572868
  141.6 8.8 %slice-start = ((s8[8388608]{0:T(1024)(128)(4,1)}), s8[4194304]{0:T(1024)(128)(4,1)S(1)}, s32[]{:S(2)}) async-start(s8[8388608]{0:T(1024)(128)(4,1)} %bitcast.123), calls=%async_computation | async-start | bytes 8388608
  145.2 5.3 %slice-start.1 = ((s8[8388608]{0:T(1024)(128)(4,1)}), s8[4194304]{0:T(1024)(128)(4,1)S(1)}, s32[]{:S(2)}) async-start(s8[8388608]{0:T(1024)(128)(4,1)} %bitcast.123), calls=%async_computation.1 | async-start | bytes 8388608
  150.5 2.7 copy-start.1
  153.2 1.6 copy-start.3
  153.2 4.5 %copy-start.7 = (bf16[256,1024]{1,0:T(8,128)(2,1)S(1)}, bf16[256,1024]{1,0:T(8,128)(2,1)}, u32[]{:S(2)}) copy-start(bf16[256,1024]{1,0:T(8,128)(2,1)} %get-tuple-element.34) | copy-start | bytes 1572868
  153.9 14.4 %copy-start = (f32[256,1024]{1,0:T(8,128)}, f32[256,1024]{1,0:T(8,128)S(1)}, u32[]{:S(2)}) copy-start(f32[256,1024]{1,0:T(8,128)S(1)} %get-tuple-element.72.grad_middle) | copy-start | bytes 3145732
  159.8 8.6 %copy-start.2 = (bf16[256,4096]{1,0:T(8,128)(2,1)S(1)}, bf16[256,4096]{1,0:T(8,128)(2,1)}, u32[]{:S(2)}) copy-start(bf16[256,4096]{1,0:T(8,128)(2,1)} %copy-done.1) | copy-start | bytes 6291460
  300.5 10.0 %copy-start.5 = (f32[2,32,4096]{2,1,0:T(8,128)S(1)}, f32[2,32,4096]{2,1,0:T(8,128)}, u32[]{:S(2)}) copy-start(f32[2,32,4096]{2,1,0:T(8,128)} %get-tuple-element.50) | copy-start | bytes 3145732
  300.5 10.9 %copy-start.4 = (f32[4,2,32,1024]{3,2,1,0:T(8,128)S(1)}, f32[4,2,32,1024]{3,2,1,0:T(8,128)}, u32[]{:S(2)}) copy-start(f32[4,2,32,1024]{3,2,1,0:T(8,128)} %get-tuple-element.51) | copy-start | bytes 3145732
